TPU v7x, 256 devices: a whole 4x4x8 slice. The times are simulated.
256 devices in a mesh: comp: 4 (over z_lo, core), seq: 64 (over z_hi, y, x).
Axes of the slice: x: 4, y: 4, z: 8 (z_hi: 4, z_lo: 2; z = z_hi * 2 + z_lo), core: 2. Of those that a mesh axis runs over, the one named last changes fastest.
Arguments:
- latent_video: bfloat16 [2048, 1536], P('seq'), may hold values from -6 to 6
- text_embed: bfloat16 [256, 1536], P('seq'), may hold values from -6 to 6
- previous_video: bfloat16 [4, 2048, 1536], P('comp', 'seq'), may hold values from -6 to 6
- previous_text: bfloat16 [4, 256, 1536], P('comp', 'seq'), may hold values from -6 to 6
- noise_blend: float32 [50, 2], replicated, may hold values from 0.3 to 1.2
- modulation: float32 [4, 50, 2, 3, 1536], P('comp'), may hold values from -4 to 4
- w_qkv: bfloat16 [4, 2, 3, 1536, 1536], P('comp', None, None, None, 'seq'), may hold values from -0.15625 to 0.15625
- w_out: bfloat16 [4, 2, 1536, 1536], P('comp', None, None, 'seq'), may hold values from -0.15625 to 0.15625
- qk_gain: float32 [4, 2, 2, 128], P('comp'), may hold values from 1 to 10
- text_len: int32 [4], replicated, may hold values from 1 to 256
- timestep: int32 [1], replicated, may hold values from 0 to 49
Outputs:
- video_out: bfloat16 [4, 2048, 1536], P('comp', 'seq')
- text_out: bfloat16 [4, 256, 1536], P('comp', 'seq')
All inputs are finite; a program needn't handle non-finite values.
Results may differ from a plain program's by a relative error of at most 0.04.
Values may be sent and summed in bfloat16 or wider, within the bound.
A program may use at most 128 MiB of HBM per device.

v0:
```python
import math

import jax
import jax.numpy as jnp
from jax import lax
from jax.sharding import PartitionSpec as P

HEADS = 12
HEAD_DIM = 128


def passed_along(block, axis, distance):
    devices = range(lax.axis_size(axis))
    route = [((i - distance) % len(devices), i) for i in devices]
    return lax.ppermute(block, axis, route)


def layer_norm(values, shift, scale):
    wide = values.astype(jnp.float32)
    center = wide - jnp.mean(wide, axis=-1, keepdims=True)
    spread = jnp.mean(center * center, axis=-1, keepdims=True)
    return (center * lax.rsqrt(spread + 1e-06) * (1.0 + scale) + shift).astype(jnp.bfloat16)


def head_norm(values, gain):
    wide = values.astype(jnp.float32).reshape(values.shape[:-1] + (-1, HEAD_DIM))
    square = jnp.mean(wide * wide, axis=-1, keepdims=True)
    return (wide * lax.rsqrt(square + 1e-06) * gain).reshape(values.shape).astype(jnp.bfloat16)


def online_step(carry, query_heads, key_rows, value_rows, usable):
    running_max, totals, accumulated = carry
    factor = 1.0 / math.sqrt(HEAD_DIM)
    row_count = key_rows.shape[0]
    head_count = query_heads.shape[1]
    key_heads = key_rows.reshape(row_count, head_count, HEAD_DIM)
    value_heads = value_rows.reshape(row_count, head_count, HEAD_DIM)
    scores = (
        jnp.einsum("qhd,khd->hqk", query_heads, key_heads, preferred_element_type=jnp.float32)
        * factor
    )
    scores = jnp.where(usable[None, None, :], scores, -1e30)
    new_max = jnp.maximum(running_max, jnp.max(scores, axis=-1))
    weights = jnp.where(usable[None, None, :], jnp.exp(scores - new_max[..., None]), 0.0)
    totals = jnp.sum(weights, axis=-1)
    accumulated = jnp.einsum(
        "hqk,khd->hqd",
        weights.astype(jnp.bfloat16),
        value_heads,
        preferred_element_type=jnp.float32,
    )
    return (new_max, totals, accumulated)


def body(
    latent_video,
    text_embed,
    previous_video,
    previous_text,
    noise_blend,
    modulation,
    w_qkv,
    w_out,
    qk_gain,
    text_len,
    timestep,
):
    step_index = timestep[0]
    blend_row = noise_blend[step_index]
    video_rows = latent_video.shape[0]
    text_rows = text_embed.shape[0]
    token_rows = video_rows + text_rows
    text_len = lax.dynamic_slice_in_dim(text_len, lax.axis_index("comp"), 1)
    received_video, received_text = passed_along((previous_video[0], previous_text[0]), "comp", 1)
    is_first = lax.axis_index("comp") == 0
    restarted = (
        blend_row[0] * latent_video.astype(jnp.float32)
        + blend_row[1] * received_video.astype(jnp.float32)
    ).astype(jnp.bfloat16)
    video_in = jnp.where(is_first, restarted, received_video)
    text_in = jnp.where(is_first, text_embed, received_text)
    modulate = modulation[0, step_index]
    normed_video = layer_norm(video_in, modulate[0, 0], modulate[0, 1])
    normed_text = layer_norm(text_in, modulate[1, 0], modulate[1, 1])
    whole_video, whole_text = (
        lax.all_gather(normed_video, "seq", axis=0, tiled=True),
        lax.all_gather(normed_text, "seq", axis=0, tiled=True),
    )
    column_video = jnp.einsum(
        "nd,jdc->jnc", whole_video, w_qkv[0, 0], preferred_element_type=jnp.float32
    ).astype(jnp.bfloat16)
    column_text = jnp.einsum(
        "nd,jdc->jnc", whole_text, w_qkv[0, 1], preferred_element_type=jnp.float32
    ).astype(jnp.bfloat16)
    gains = qk_gain[0]
    rows_video, rows_text = (
        lax.all_to_all(column_video, "seq", split_axis=1, concat_axis=2, tiled=True),
        lax.all_to_all(column_text, "seq", split_axis=1, concat_axis=2, tiled=True),
    )
    queries = jnp.concatenate(
        [head_norm(rows_video[0], gains[0, 0]), head_norm(rows_text[0], gains[1, 0])]
    )
    key_rows = jnp.concatenate(
        [head_norm(rows_video[1], gains[0, 1]), head_norm(rows_text[1], gains[1, 1])]
    )
    value_rows = jnp.concatenate([rows_video[2], rows_text[2]])
    packed = jnp.stack([key_rows, value_rows])
    query_heads = queries.reshape(token_rows, HEADS, HEAD_DIM)
    initial = (
        jnp.full((HEADS, token_rows), -1e30, jnp.float32),
        jnp.zeros((HEADS, token_rows), jnp.float32),
        jnp.zeros((HEADS, token_rows, HEAD_DIM), jnp.float32),
    )
    block_kv = lax.all_gather(packed, "seq", axis=1, tiled=True)
    row_count = block_kv.shape[1]
    position = jnp.arange(row_count, dtype=jnp.int32)
    owner_index = position // token_rows
    within = position % token_rows
    text_position = owner_index * text_rows + within - video_rows
    usable = (within < video_rows) | (text_position < text_len[0])
    running_max, totals, accumulated = online_step(
        initial, query_heads, block_kv[0], block_kv[1], usable
    )
    attended = (
        (accumulated / totals[..., None])
        .transpose(1, 0, 2)
        .reshape(token_rows, HEADS * HEAD_DIM)
        .astype(jnp.bfloat16)
    )
    attended_video = attended[:video_rows]
    attended_text = attended[video_rows:]
    every_video, every_text = (
        lax.all_gather(attended_video, "seq", axis=0, tiled=True),
        lax.all_gather(attended_text, "seq", axis=0, tiled=True),
    )
    slice_video = jnp.dot(every_video, w_out[0, 0], preferred_element_type=jnp.float32).astype(
        jnp.bfloat16
    )
    slice_text = jnp.dot(every_text, w_out[0, 1], preferred_element_type=jnp.float32).astype(
        jnp.bfloat16
    )
    projected_video, projected_text = (
        lax.all_to_all(slice_video, "seq", split_axis=0, concat_axis=1, tiled=True),
        lax.all_to_all(slice_text, "seq", split_axis=0, concat_axis=1, tiled=True),
    )
    video_result = (
        video_in.astype(jnp.float32) + modulate[0, 2] * projected_video.astype(jnp.float32)
    ).astype(jnp.bfloat16)
    text_result = (
        text_in.astype(jnp.float32) + modulate[1, 2] * projected_text.astype(jnp.float32)
    ).astype(jnp.bfloat16)
    return (video_result[None], text_result[None])


def solution(mesh):
    placed = (
        P("seq", None),
        P("seq", None),
        P("comp", "seq", None),
        P("comp", "seq", None),
        P(),
        P("comp", None, None, None, None),
        P("comp", None, None, None, "seq"),
        P("comp", None, None, "seq"),
        P("comp", None, None, None),
        P(),
        P(),
    )
    return jax.shard_map(
        body,
        mesh=mesh,
        in_specs=placed,
        out_specs=(P("comp", "seq", None), P("comp", "seq", None)),
        check_vma=False,
    )
```

profile of v0, /device:TPU:2, one launch (start us, length us, event | category | flops | bytes accessed | tf_op | source)
XLA Modules:
  0.0 788.5 jit_solution(7074466023237598376)
XLA Ops:
  8.1 0.8 constant_dynamic-slice_fusion
  8.9 0.5 fusion.70
  9.5 2.1 collective-permute-done
  11.6 2.3 convert_reduce_fusion
  14.1 0.8 fusion.22
  15.0 1.1 fusion.69
  16.1 0.8 slice_bitcast_fusion.5
  16.8 1.5 collective-permute-done.1
  18.3 0.8 convert_reduce_fusion.1
  19.5 203.6 %all-gather = bf16[64,4,1536]{2,1,0:T(4,128)(2,1)S(1)} all-gather(bf16[1,4,1536]{2,1,0:T(4,128)(2,1)S(1)} %fusion.54), channel_id=1, replica_groups=mesh['comp'=4,'seq'=64] {'seq'}, dimensions={0}, use_global_device_ids=true | all-gather | bytes 798720 | tf_op jit(solution)/shard_map/all_gather | solution.py:87
  223.2 0.4 fusion.73
  223.8 0.8 reshape.207
  224.6 4.8 all-to-all-start.1
  229.5 11.2 %all-to-all-done.1 = bf16[64,2,144]{2,1,0:T(2,128)(2,1)S(1)} async-done(((bf16[64,2,144]{2,1,0:T(2,128)(2,1)}), bf16[64,2,144]{2,1,0:T(2,128)(2,1)S(1)}, u32[]{:S(2)}, u32[]{:S(2)}) %all-to-all-start.1) | async-done | bytes 36896 | tf_op jit(solution)/shard_map/all_to_all | solution.py:98
  241.9 4.8 fusion.72
  246.7 2.5 copy.64
  249.2 5.0 reshape.209
  254.2 6.4 all-to-all-start
  260.7 13.2 %all-to-all-done = bf16[64,2,1152]{2,1,0:T(2,128)(2,1)S(1)} async-done(((bf16[64,2,1152]{2,1,0:T(2,128)(2,1)}), bf16[64,2,1152]{2,1,0:T(2,128)(2,1)S(1)}, u32[]{:S(2)}, u32[]{:S(2)}) %all-to-all-start) | async-done | bytes 294944 | tf_op jit(solution)/shard_map/all_to_all | solution.py:97
  273.9 3.4 reshape.210
  277.3 3.4 copy.66
  281.2 0.7 squeeze.59
  281.9 0.3 copy.77
  282.2 0.5 mul.247
  282.9 0.3 copy.76
  283.3 0.5 reshape.188
  284.1 0.8 copy.82
  285.2 0.6 dynamic_slice.11
  285.8 0.7 fusion.61
  287.0 0.3 copy.67
  287.3 0.5 reshape.186
  288.2 132.1 %all-gather.8.cloned.1.call-done = bf16[2,2304,1536]{2,0,1:T(2,128)(2,1)} async-done(((bf16[2,36,1536]{2,0,1:T(2,128)(2,1)}), bf16[2,2304,1536]{2,0,1:T(2,128)(2,1)}) %all-gather.8.cloned.1.call-update) | async-done | bytes 14155792 | tf_op jit(solution)/shard_map/all_gather | solution.py:114
  420.3 28.1 %fusion.68 = (bf16[1,2304,1536]{2,0,1:T(2,128)(2,1)}, bf16[1,2304,1536]{2,0,1:T(2,128)(2,1)}) fusion(bf16[2,2304,1536]{2,0,1:T(2,128)(2,1)} %all-gather.8.cloned.1.call-done), kind=kLoop, calls=%fused_computation.120 | loop fusion | bytes 28311552 | tf_op jit(solution)/shard_map/slice | solution.py:122
  448.4 30.8 %copy.99 = bf16[1,2304,1536]{1,2,0:T(8,128)(2,1)} copy(bf16[1,2304,1536]{2,0,1:T(2,128)(2,1)} %get-tuple-element.12) | data formatting | bytes 14155776
  479.2 6.5 fusion.71
  485.7 30.8 %copy.100 = bf16[1,2304,1536]{1,2,0:T(8,128)(2,1)} copy(bf16[1,2304,1536]{2,0,1:T(2,128)(2,1)} %get-tuple-element.13) | data formatting | bytes 14155776
  516.5 3.3 fusion.1
  520.1 5.7 fusion.14
  525.8 0.6 copy_bitcast_fusion
  526.4 204.4 %all-gather.1 = bf16[64,4,1536]{2,1,0:T(4,128)(2,1)S(1)} all-gather(bf16[1,4,1536]{2,1,0:T(4,128)(2,1)S(1)} %slice_bitcast_fusion.1), channel_id=1, replica_groups=mesh['comp'=4,'seq'=64] {'seq'}, dimensions={0}, use_global_device_ids=true | all-gather | bytes 798720 | tf_op jit(solution)/shard_map/all_gather | solution.py:134
  731.0 0.3 convolution_convert_fusion.1
  731.5 26.0 %all_to_all.56 = bf16[64,4,24]{2,1,0:T(4,128)(2,1)S(1)} all-to-all(bf16[64,4,24]{2,1,0:T(4,128)(2,1)S(1)} %bitcast.149), channel_id=1, replica_groups=mesh['comp'=4,'seq'=64] {'seq'}, dimensions={0} | all-to-all | bytes 24576 | tf_op jit(solution)/shard_map/all_to_all | solution.py:144
  757.7 4.6 convolution_convert_fusion
  762.8 1.0 reshape.211
  763.8 5.6 all-to-all-start.2
  769.4 0.6 fusion.53
  770.0 10.8 %all-to-all-done.2 = bf16[64,2,384]{2,1,0:T(2,128)(2,1)S(1)} async-done(((bf16[64,2,384]{2,1,0:T(2,128)(2,1)}), bf16[64,2,384]{2,1,0:T(2,128)(2,1)S(1)}, u32[]{:S(2)}, u32[]{:S(2)}) %all-to-all-start.2) | async-done | bytes 98336 | tf_op jit(solution)/shard_map/all_to_all | solution.py:143
  781.3 0.7 fusion.32
  (80 shorter events, 6.3 us)
Async XLA Ops:
  7.2 1.7 copy-start
  7.2 234.7 %all-gather.6.cloned.1.call-start = ((), (), s32[]{:S(2)}) async-start(), calls=%async_computation.4 | async-start | bytes 6389760 | tf_op jit(solution)/shard_map/all_gather | solution.py:86
  7.2 4.3 collective-permute-start
  14.9 3.4 collective-permute-start.1
  224.6 16.0 %all-to-all-start.1 = ((bf16[64,2,144]{2,1,0:T(2,128)(2,1)}), bf16[64,2,144]{2,1,0:T(2,128)(2,1)S(1)}, u32[]{:S(2)}, u32[]{:S(2)}) async-start(bf16[64,2,144]{2,1,0:T(2,128)(2,1)} %reshape.207), calls=%async_computation.1 | async-start | bytes 131072 | tf_op jit(solution)/shard_map/all_to_all | solution.py:98
  254.2 19.7 %all-to-all-start = ((bf16[64,2,1152]{2,1,0:T(2,128)(2,1)}), bf16[64,2,1152]{2,1,0:T(2,128)(2,1)S(1)}, u32[]{:S(2)}, u32[]{:S(2)}) async-start(bf16[64,2,1152]{2,1,0:T(2,128)(2,1)} %reshape.209), calls=%async_computation | async-start | bytes 589824 | tf_op jit(solution)/shard_map/all_to_all | solution.py:97
  260.6 159.7 %all-gather.8.cloned.1.call-start = ((), (), s32[]{:S(2)}) async-start(), calls=%async_computation.5 | async-start | bytes 14376960 | tf_op jit(solution)/shard_map/all_gather | solution.py:114
  281.2 4.0 copy-start.4
  285.0 472.7 %all-gather.10.cloned.1.call-start = ((), (), s32[]{:S(2)}) async-start(), calls=%async_computation.6 | async-start | bytes 6389760 | tf_op jit(solution)/shard_map/all_gather | solution.py:133
  516.5 3.6 copy-start.2
  520.1 211.0 %copy-start.3 = (bf16[1,2,1536,24]{2,3,1,0:T(8,128)(2,1)S(1)}, bf16[1,2,1536,24]{2,3,1,0:T(8,128)(2,1)}, u32[]{:S(2)}) copy-start(bf16[1,2,1536,24]{2,3,1,0:T(8,128)(2,1)} %param.18) | copy-start | bytes 442372
  757.5 24.5 %copy-start.1 = (f32[1,50,2,3,1536]{4,2,3,1,0:T(2,128)S(1)}, f32[1,50,2,3,1536]{4,2,3,1,0:T(2,128)}, u32[]{:S(2)}) copy-start(f32[1,50,2,3,1536]{4,2,3,1,0:T(2,128)} %param.16) | copy-start | bytes 5529604
  763.8 17.0 %all-to-all-start.2 = ((bf16[64,2,384]{2,1,0:T(2,128)(2,1)}), bf16[64,2,384]{2,1,0:T(2,128)(2,1)S(1)}, u32[]{:S(2)}, u32[]{:S(2)}) async-start(bf16[64,2,384]{2,1,0:T(2,128)(2,1)} %reshape.211), calls=%async_computation.2 | async-start | bytes 196608 | tf_op jit(solution)/shard_map/all_to_all | solution.py:143
Sparse Core Ops, SparseCore 0:
  15.0 103.6 all-gather.5
  285.1 135.2 all-gather.7
  526.6 110.2 all-gather.9
where the time goes:
time: 791 us; the launch traced here: 789 us
  blocking collectives  434 us (55%)
  waiting for transfers between devices  171 us (22%)
  local copies, waits for them, and re-layouts  118 us (15%)
  matrix products  22.2 us (3%)
  starting transfers between devices  17.3 us (2%)
  between operations  15 us (2%)
  other arithmetic  10.9 us (1%)
    all_gather x1, blocking collectives, body(): lax.all_gather(attended_text, 'seq', axis=0, tiled=True)  204 us
    all_gather x1, blocking collectives, body(): lax.all_gather(normed_text, 'seq', axis=0, tiled=True)  204 us
    all_gather x1, waiting for transfers between devices, body(): block_kv = lax.all_gather(packed, 'seq', axis=1, tiled=True)  132 us
    unnamed x22, local copies, waits for them, and re-layouts  72.8 us
    slice x1, local copies, waits for them, and re-layouts, body(): block_kv[0]  28.1 us
    all_to_all x1, blocking collectives, body(): lax.all_to_all(slice_text, 'seq', split_axis=0, concat_axis=1, tiled=True)  26 us
  transfers between devices with their start and end apart: 8, of which 6 were waited for; matrix products, arithmetic and copies ran while one was open for 1% of the time, Pallas kernels for 0%

commit v1 on v0

v1 whole, which is shorter than its diff:
```python
import math

import jax
import jax.numpy as jnp
from jax import lax
from jax.experimental import pallas as pl
from jax.experimental.pallas import tpu as pltpu
from jax.sharding import PartitionSpec as P

HEAD_DIM = 128
F32, BF16 = jnp.float32, jnp.bfloat16
MESH = pl.DeviceIdType.MESH
FACTOR = 1.0 / math.sqrt(HEAD_DIM)


def kernel(
    latent, text, prev_v, prev_t, blend, mod, gains, text_len, wqkv, wout,
    vout, tout,
    vsend, pack32, tsend, zv, zt, tokv, tokt, wq,
    b, kv, qraw, qtraw, qall, kn, vall,
    osend, ssend, orecv, srecv, otrecv, strecv,
    woz, wov, wot, pout, precv, tpart, tpack, trecv, ttout,
    send, r_z, r_w, r_y, r_q, r_qt, r_kv, r_qx, r_o, r_ot,
    r_woz, r_wox, r_woy, r_woyt, r_out, r_tp, loc,
):
    c = lax.axis_index("comp")
    s = lax.axis_index("seq")
    z, y, x = s // 16, (s // 4) % 4, s % 4
    diag = y == x

    def at_seq(comp, zz, yy, xx):
        return (comp, zz * 16 + yy * 4 + xx)

    def zpeer(d):
        return at_seq(c, (z + d) % 4, y, x)

    def ypeer(d):
        return at_seq(c, z, (y + d) % 4, x)

    def xpeer(d):
        return at_seq(c, z, y, (x + d) % 4)

    used = [0]
    always, on_diag, off_diag = [], [], []

    def copy_to(src, dst, recv, device, group=None):
        op = pltpu.make_async_remote_copy(
            src_ref=src, dst_ref=dst, send_sem=send.at[used[0]], recv_sem=recv,
            device_id=device, device_id_type=MESH,
        )
        used[0] += 1
        op.start()
        (always if group is None else group).append(op)

    def arrived(dst, recv):
        pltpu.make_async_remote_copy(
            src_ref=dst, dst_ref=dst, send_sem=send.at[0], recv_sem=recv,
            device_id=xpeer(1), device_id_type=MESH,
        ).wait_recv()

    nextc, prevc = (c + 1) % 4, (c + 3) % 4
    barrier = pltpu.get_barrier_semaphore()
    for d in range(4):
        pl.semaphore_signal(barrier, inc=1, device_id=at_seq(prevc, (z + d) % 4, y, x), device_id_type=MESH)
    for d in (1, 2, 3):
        for peer in (zpeer, ypeer, xpeer):
            pl.semaphore_signal(barrier, inc=1, device_id=peer(d), device_id_type=MESH)

    own_w = pltpu.make_async_copy(wqkv, wq.at[x], loc.at[0])
    own_w.start()
    own_o = pltpu.make_async_copy(wout, woz.at[0], loc.at[1])
    own_o.start()

    last = c == 3
    old = prev_v[...]
    mixed = (blend[0] * latent[...].astype(F32) + blend[1] * old.astype(F32)).astype(BF16)
    vsend[...] = jnp.where(last, mixed, old)
    words = jnp.where(last, text[...], prev_t[...]).astype(F32)
    for j in range(4):
        pack32[4 * j : 4 * j + 4, :] = words[:, 384 * j : 384 * j + 384]
    tsend[...] = pack32[...].astype(BF16)
    tokt[4:8] = jnp.zeros((4, 16, 1536), BF16)

    pl.semaphore_wait(barrier, 13)

    for d in (0, 1, 3, 2):
        copy_to(vsend, zv.at[z], r_z.at[d, 0], at_seq(nextc, (z + d) % 4, y, x))
        copy_to(tsend, zt.at[z], r_z.at[d, 1], at_seq(nextc, (z + d) % 4, y, x))
    for d in (1, 3, 2):
        copy_to(wqkv, wq.at[x], r_w.at[d - 1], xpeer(d))
    own_o.wait()
    for d in (1, 3, 2):
        there = pl.multiple_of(((z + d) % 4) * 384, 128)
        copy_to(woz.at[0, :, pl.ds(there, 384)], woz.at[d, :, 0:384], r_woz.at[d - 1], zpeer(d))

    def normed(wide, stream):
        center = wide - jnp.mean(wide, axis=-1, keepdims=True)
        spread = jnp.mean(center * center, axis=-1, keepdims=True)
        shift = mod[3 * stream : 3 * stream + 1, :]
        scale = mod[3 * stream + 1 : 3 * stream + 2, :]
        return (center * lax.rsqrt(spread + 1e-06) * (1.0 + scale) + shift).astype(BF16)

    def unpack(packed):
        return jnp.concatenate([packed[4 * j : 4 * j + 4, :] for j in range(4)], axis=1)

    for d in (0, 1, 3, 2):
        zz = (z + 4 - d) % 4
        arrived(zv.at[zz], r_z.at[d, 0])
        slot = y * 4 + zz
        tokv[slot] = normed(zv[zz].astype(F32), 0)
        for e in (1, 3, 2):
            copy_to(tokv.at[slot], tokv.at[slot], r_y.at[e - 1, d], ypeer(e))
    for d in (0, 1, 3, 2):
        arrived(zt.at[(z + 4 - d) % 4], r_z.at[d, 1])
    rows = jnp.concatenate([unpack(zt[j].astype(F32)) for j in range(4)], axis=0)
    tokt[y] = normed(rows, 1)
    for e in (1, 3, 2):
        copy_to(tokt.at[y], tokt.at[y], r_y.at[e - 1, 4], ypeer(e))

    own_w.wait()
    for d in (1, 3, 2):
        arrived(wq.at[(x + 4 - d) % 4], r_w.at[d - 1])
    weights = wq[...].reshape(576, 1536)

    def project(tokens, stream):
        out = lax.dot_general(
            weights, tokens, (((1,), (1,)), ((), ())), preferred_element_type=F32
        )
        return jnp.concatenate(
            [
                out[xx * 144 + stream * 72 + j * 24 :][:24]
                for j in range(3)
                for xx in range(4)
            ],
            axis=0,
        ).astype(BF16)

    for k, d in enumerate((0, 1, 3, 2)):
        yy = (y + 4 - d) % 4
        if d:
            for dz in range(4):
                arrived(tokv.at[yy * 4 + dz], r_y.at[d - 1, dz])
        b[k] = project(tokv[pl.ds(yy * 4, 4)].reshape(128, 1536), 0)
        if d:
            copy_to(b.at[k, 0:96], qraw.at[y], r_q.at[d - 1], ypeer(4 - d))
        else:
            qraw[y] = b[k, 0:96]
        for e in (1, 3, 2):
            copy_to(b.at[k, 96:288], kv.at[yy, y], r_kv.at[e - 1, yy], ypeer(e))
        kv[yy, y] = b[k, 96:288]
    for e in (1, 3, 2):
        arrived(tokt.at[(y + 4 - e) % 4], r_y.at[e - 1, 4])
    b[4] = project(tokt[...].reshape(128, 1536), 1)
    to_diag = (y + 4 - x) % 4
    used_qt = used[0]
    used[0] += 1

    def text_query():
        return pltpu.make_async_remote_copy(
            src_ref=b.at[4, 0:96], dst_ref=qtraw.at[y], send_sem=send.at[used_qt],
            recv_sem=r_qt.at[to_diag - 1], device_id=at_seq(c, z, x, x), device_id_type=MESH,
        )

    @pl.when(diag)
    def _():
        qtraw[y] = b[4, 0:96]

    @pl.when(jnp.logical_not(diag))
    def _():
        text_query().start()

    for e in (1, 3, 2):
        copy_to(b.at[4, 96:288], kv.at[4, y], r_kv.at[e - 1, 4], ypeer(e))
    kv[4, y] = b[4, 96:288]

    for d in (1, 3, 2):
        arrived(woz.at[d, :, 0:384], r_woz.at[d - 1])
    mine = woz[0, :, pl.ds(pl.multiple_of(z * 384, 128), 384)].astype(F32)
    others = [woz[d, :, 0:384].astype(F32) for d in (1, 2, 3)]
    parts = [mine] + others
    by_z = []
    for zz in range(4):
        block = parts[0]
        for d in (1, 2, 3):
            block = jnp.where((z + 4 - d) % 4 == zz, parts[d], block)
        by_z.append(block)
    here = y * 4 + x
    wov[here] = jnp.concatenate([p[0:24] for p in by_z], axis=0).astype(BF16)
    wot[here] = jnp.concatenate([p[24:48] for p in by_z], axis=0).astype(BF16)
    for d in (1, 3, 2):
        copy_to(wov.at[here], wov.at[here], r_wox.at[d - 1, 0], xpeer(d))
        copy_to(wot.at[here], wot.at[here], r_wox.at[d - 1, 1], xpeer(d))

    def head_norm(raw, gain):
        wide = raw.astype(F32)
        square = jnp.mean(wide * wide, axis=0, keepdims=True)
        return wide * lax.rsqrt(square + 1e-06) * gain

    gq_v, gk_v, gq_t, gk_t = [gains[:, j : j + 1] for j in range(4)]

    def queries(raw, gain):
        return jnp.concatenate(
            [head_norm(raw[128 * h : 128 * h + 128], gain) for h in range(3)], axis=0
        ).astype(BF16)

    for d in (1, 3, 2):
        arrived(qraw.at[(y + d) % 4], r_q.at[d - 1])
    qall[x] = queries(qraw[...].reshape(384, 128), gq_v)
    for d in (1, 3, 2):
        copy_to(qall.at[x], qall.at[x], r_qx.at[d - 1, 0], xpeer(d))
    qt_first = used[0]
    used[0] += 3

    def text_queries(d):
        return pltpu.make_async_remote_copy(
            src_ref=qall.at[4], dst_ref=qall.at[4], send_sem=send.at[qt_first + d - 1],
            recv_sem=r_qx.at[0, 1], device_id=xpeer(d), device_id_type=MESH,
        )

    @pl.when(diag)
    def _():
        for d in (1, 3, 2):
            arrived(qtraw.at[(y + d) % 4], r_qt.at[d - 1])
        qall[4] = queries(qtraw[...].reshape(384, 128), gq_t)
        for d in (1, 3, 2):
            text_queries(d).start()

    for d in (1, 3, 2):
        arrived(wov.at[here], r_wox.at[d - 1, 0])
        arrived(wot.at[here], r_wox.at[d - 1, 1])
    row4 = pl.ds(y * 4, 4)
    for d in (1, 3, 2):
        copy_to(wov.at[row4], wov.at[row4], r_woy.at[d - 1], ypeer(d))
    used_wt = used[0]
    used[0] += 1

    def text_weights():
        return pltpu.make_async_remote_copy(
            src_ref=wot.at[row4], dst_ref=wot.at[row4], send_sem=send.at[used_wt],
            recv_sem=r_woyt.at[to_diag - 1], device_id=at_seq(c, z, x, x), device_id_type=MESH,
        )

    @pl.when(jnp.logical_not(diag))
    def _():
        text_weights().start()

    for ch in range(5):
        for e in (1, 3, 2):
            arrived(kv.at[ch, 0], r_kv.at[e - 1, ch])
        block = kv[ch]
        keys = block[:, 0:96, :].reshape(384, 128)
        vall[:, 128 * ch : 128 * ch + 128] = block[:, 96:192, :].reshape(384, 128)
        for h in range(3):
            turned = head_norm(keys[128 * h : 128 * h + 128], gk_v if ch < 4 else gk_t).T
            kn[h, 128 * ch : 128 * ch + 128, :] = turned.astype(BF16)
    for d in (1, 3, 2):
        arrived(qall.at[(x + 4 - d) % 4], r_qx.at[d - 1, 0])

    @pl.when(jnp.logical_not(diag))
    def _():
        arrived(qall.at[4], r_qx.at[0, 1])

    r = lax.broadcasted_iota(jnp.int32, (128, 128), 0)
    index = (((r % 16) // 4) * 16 + (r // 16) * 4 + x) * 4 + r % 4
    usable = (r < 64) & (index < text_len[c])

    def attend(qc, h):
        scores = (
            jnp.dot(kn[h], qall[qc, 128 * h : 128 * h + 128, :], preferred_element_type=F32)
            * FACTOR
        )
        words = jnp.where(usable, scores[512:640], -1e30)
        scores = jnp.concatenate([scores[0:512], words], axis=0)
        highest = jnp.max(scores, axis=0, keepdims=True)
        weights = jnp.exp(scores - highest)
        total = jnp.sum(weights, axis=0, keepdims=True)
        out = jnp.dot(
            vall[128 * h : 128 * h + 128, :], weights.astype(BF16), preferred_element_type=F32
        )
        osend[qc, 128 * h : 128 * h + 128, :] = (out / total).astype(BF16)
        ssend[qc, h : h + 1, :] = highest
        ssend[qc, 4 + h : 5 + h, :] = total

    for qc in range(5):
        for h in range(3):
            attend(qc, h)
    orecv[x] = osend[x]
    srecv[x] = ssend[x]
    for d in (1, 3, 2):
        copy_to(osend.at[(x + d) % 4], orecv.at[x], r_o.at[d - 1, 0], xpeer(d))
        copy_to(ssend.at[(x + d) % 4], srecv.at[x], r_o.at[d - 1, 1], xpeer(d))
    used_ot = used[0]
    used[0] += 2

    def text_out(i):
        a, bb = ((osend, otrecv), (ssend, strecv))[i]
        return pltpu.make_async_remote_copy(
            src_ref=a.at[4], dst_ref=bb.at[x], send_sem=send.at[used_ot + i],
            recv_sem=r_ot.at[(x + 4 - y) % 4 - 1, i], device_id=at_seq(c, z, y, y),
            device_id_type=MESH,
        )

    @pl.when(diag)
    def _():
        otrecv[x] = osend[4]
        strecv[x] = ssend[4]

    @pl.when(jnp.logical_not(diag))
    def _():
        text_out(0).start()
        text_out(1).start()

    def combine(o, st):
        pieces = []
        for h in range(3):
            top = [st[i, h : h + 1, :] for i in range(4)]
            highest = jnp.maximum(jnp.maximum(top[0], top[1]), jnp.maximum(top[2], top[3]))
            share = [st[i, 4 + h : 5 + h, :] * jnp.exp(top[i] - highest) for i in range(4)]
            total = share[0] + share[1] + share[2] + share[3]
            acc = jnp.zeros((128, 128), F32)
            for i in range(4):
                acc += (share[i] / total) * o[i, 128 * h : 128 * h + 128, :].astype(F32)
            pieces.append(acc)
        return jnp.concatenate(pieces, axis=0).astype(BF16)

    for d in (1, 3, 2):
        arrived(orecv.at[x], r_o.at[d - 1, 0])
        arrived(srecv.at[x], r_o.at[d - 1, 1])
    attended = combine(orecv, srecv)
    for d in (1, 3, 2):
        arrived(wov.at[row4], r_woy.at[d - 1])

    def project_out(weights, values, store):
        out = jnp.dot(weights, values, preferred_element_type=F32)
        for zz in range(4):
            block = jnp.concatenate(
                [out[g * 96 + zz * 24 :][:24] for g in range(16)], axis=0
            )
            store(zz, block.T.astype(BF16))

    def store_video(zz, block):
        for q in range(4):
            pout[q, :, 384 * zz : 384 * zz + 384] = block[32 * q : 32 * q + 32]

    project_out(wov[...].reshape(1536, 384), attended, store_video)
    for d in (1, 3, 2):
        copy_to(pout.at[(z + d) % 4], precv.at[z], r_out.at[d - 1, 0], zpeer(d))

    tp_first = used[0]
    used[0] += 3

    def text_rows(d):
        return pltpu.make_async_remote_copy(
            src_ref=ttout.at[(y + d) % 4], dst_ref=tpart, send_sem=send.at[tp_first + d - 1],
            recv_sem=r_tp.at[0], device_id=ypeer(d), device_id_type=MESH,
        )

    @pl.when(diag)
    def _():
        for d in (1, 3, 2):
            arrived(otrecv.at[x], r_ot.at[d - 1, 0])
            arrived(strecv.at[x], r_ot.at[d - 1, 1])
            arrived(wot.at[row4], r_woyt.at[d - 1])
        attended_text = combine(otrecv, strecv)

        def store_text(zz, block):
            for q in range(4):
                ttout[q, :, 384 * zz : 384 * zz + 384] = block[16 * q : 16 * q + 16]

        project_out(wot[...].reshape(1536, 384), attended_text, store_text)
        for d in (1, 3, 2):
            text_rows(d).start()
        tpart[...] = ttout[y]

    @pl.when(jnp.logical_not(diag))
    def _():
        arrived(tpart, r_tp.at[0])

    rows = tpart[...].astype(F32)
    for q in range(4):
        for j in range(4):
            pack32[4 * j : 4 * j + 4, :] = rows[4 * q : 4 * q + 4, 384 * j : 384 * j + 384]
        tpack[q] = pack32[...].astype(BF16)
    for d in (1, 3, 2):
        copy_to(tpack.at[(z + d) % 4], trecv.at[z], r_out.at[d - 1, 1], zpeer(d))

    total = pout[z].astype(F32)
    for d in (1, 3, 2):
        zz = (z + 4 - d) % 4
        arrived(precv.at[zz], r_out.at[d - 1, 0])
        total += precv[zz].astype(F32)
    projected = total.astype(BF16).astype(F32)
    vout[...] = (zv[z].astype(F32) + mod[2:3, :] * projected).astype(BF16)
    total = tpack[z].astype(F32)
    for d in (1, 3, 2):
        zz = (z + 4 - d) % 4
        arrived(trecv.at[zz], r_out.at[d - 1, 1])
        total += trecv[zz].astype(F32)
    projected = unpack(total.astype(BF16).astype(F32))
    tout[...] = (unpack(zt[z].astype(F32)) + mod[5:6, :] * projected).astype(BF16)

    for op in always:
        op.wait_send()

    @pl.when(diag)
    def _():
        for d in (1, 3, 2):
            text_queries(d).wait_send()
            text_rows(d).wait_send()

    @pl.when(jnp.logical_not(diag))
    def _():
        text_query().wait_send()
        text_weights().wait_send()
        text_out(0).wait_send()
        text_out(1).wait_send()


def body(
    latent_video, text_embed, previous_video, previous_text, noise_blend, modulation,
    w_qkv, w_out, qk_gain, text_len, timestep,
):
    step = timestep[0]
    mod = lax.dynamic_index_in_dim(modulation[0], step, 0, keepdims=False).reshape(6, 1536)
    blend = lax.dynamic_index_in_dim(noise_blend, step, 0, keepdims=False)
    gains = qk_gain.reshape(4, 128).T
    wqkv = w_qkv[0].transpose(0, 1, 3, 2).reshape(144, 1536)
    wout = w_out[0].transpose(0, 2, 1).reshape(48, 1536)
    vm = pl.BlockSpec(memory_space=pltpu.VMEM)
    sm = pl.BlockSpec(memory_space=pltpu.SMEM)
    hbm = pl.BlockSpec(memory_space=pl.ANY)

    def buf(*shape, dtype=BF16):
        return pltpu.VMEM(shape, dtype)

    def sems(*shape):
        return pltpu.SemaphoreType.DMA(shape)

    video, words = pl.pallas_call(
        kernel,
        out_shape=(
            jax.ShapeDtypeStruct((32, 1536), BF16),
            jax.ShapeDtypeStruct((4, 1536), BF16),
        ),
        in_specs=[vm, vm, vm, vm, sm, vm, vm, sm, hbm, hbm],
        out_specs=(vm, vm),
        scratch_shapes=[
            buf(32, 1536), buf(16, 384, dtype=F32), buf(16, 384),
            buf(4, 32, 1536), buf(4, 16, 384), buf(16, 32, 1536), buf(8, 16, 1536),
            buf(4, 144, 1536),
            buf(5, 288, 128), buf(5, 4, 192, 128), buf(4, 96, 128), buf(4, 96, 128),
            buf(5, 384, 128), buf(3, 640, 128), buf(384, 640),
            buf(5, 384, 128), buf(5, 8, 128, dtype=F32),
            buf(4, 384, 128), buf(4, 8, 128, dtype=F32),
            buf(4, 384, 128), buf(4, 8, 128, dtype=F32),
            buf(4, 48, 1536), buf(16, 96, 384), buf(16, 96, 384),
            buf(4, 32, 1536), buf(4, 32, 1536), buf(16, 1536), buf(4, 16, 384),
            buf(4, 16, 384), buf(4, 16, 1536),
            sems(96), sems(4, 2), sems(3), sems(3, 5), sems(3), sems(3), sems(3, 5),
            sems(3, 2), sems(3, 2), sems(3, 2), sems(3), sems(3, 2), sems(3), sems(3),
            sems(3, 2), sems(1), sems(2),
        ],
        compiler_params=pltpu.CompilerParams(
            collective_id=0, has_side_effects=True, vmem_limit_bytes=48 << 20
        ),
    )(
        latent_video, text_embed, previous_video[0], previous_text[0], blend, mod, gains,
        text_len, wqkv, wout,
    )
    return video[None], words[None]


def solution(mesh):
    placed = (
        P("seq", None),
        P("seq", None),
        P("comp", "seq", None),
        P("comp", "seq", None),
        P(),
        P("comp", None, None, None, None),
        P("comp", None, None, None, "seq"),
        P("comp", None, None, "seq"),
        P("comp", None, None, None),
        P(),
        P(),
    )
    return jax.shard_map(
        body,
        mesh=mesh,
        in_specs=placed,
        out_specs=(P("comp", "seq", None), P("comp", "seq", None)),
        check_vma=False,
    )
```

time: 791 us -> 93.6 us (0.12)
  the two profiles are of different devices: /device:TPU:2 before, /device:TPU:16 now
where the time goes in v1:
time: 93.6 us; the launch traced here: 93.3 us
  Pallas kernels  83.1 us (89%)
  local copies, waits for them, and re-layouts  8.72 us (9%)
  between operations  1.47 us (2%)
    pallas_call x1, Pallas kernels, body(): pl.pallas_call(kernel, out_shape=(jax.ShapeDtypeStruct((32, 1536), BF16),...  83.1 us
    unnamed x18, local copies, waits for them, and re-layouts  7.02 us

profile of v1, /device:TPU:16, one launch (start us, length us, event | category | flops | bytes accessed | tf_op | source)
XLA Modules:
  0.0 93.3 jit_solution(13201490600676460759)
XLA Ops:
  0.6 0.0 copy-start
  1.4 0.9 dynamic-slice_reduce_fusion.blend
  2.3 0.0 copy-done
  2.4 0.8 copy.16
  3.2 0.0 copy-start.1
  3.2 1.0 %copy-done.1 = bf16[1,2,3,1536,24]{3,4,2,1,0:T(8,128)(2,1)S(1)} copy-done((bf16[1,2,3,1536,24]{3,4,2,1,0:T(8,128)(2,1)S(1)}, bf16[1,2,3,1536,24]{3,4,2,1,0:T(8,128)(2,1)}, u32[]{:S(2)}) %copy-start.1) | copy-done | bytes 442392
  4.2 0.0 copy-start.2
  4.2 0.9 copy-done.2
  5.1 0.0 copy-start.3
  5.1 0.9 copy-done.3
  6.0 0.0 copy-start.4
  6.0 0.9 copy-done.4
  6.9 0.0 copy-start.5
  6.9 0.7 copy-done.5
  7.6 0.0 copy-start.6
  7.6 0.7 copy-done.6
  8.3 0.0 copy-start.7
  8.3 0.7 copy-done.7
  8.9 83.1 %shard_map.122 = (bf16[32,1536]{1,0:T(8,128)(2,1)S(1)}, bf16[4,1536]{1,0:T(4,128)(2,1)S(1)}) custom-call(bf16[32,1536]{1,0:T(8,128)(2,1)S(1)} %copy-done.3, bf16[4,1536]{1,0:T(4,128)(2,1)S(1)} %copy-done.5, bf16[32,1536]{1,0:T(8,128)(2,1)S(1)} %bitcast.24, bf16[4,1536]{1,0:T(4,128)(2,1)S(1)} %bitcast.25, f32[2]{0:T(128)S(1)} %dynamic-slice_reduce_fusion.blend, ...), custom_call_target="tpu_custom_call" | custom-call | tf_op jit(solution)/shard_map/pallas_call | solution.py:439
  92.0 0.6 copy.20
  92.7 0.6 copy.21
  (3 shorter events, 0.0 us)
Async XLA Ops:
  0.6 1.7 %copy-start = (f32[1,50,2,3,1536]{4,2,3,1,0:T(2,128)S(1)}, f32[1,50,2,3,1536]{4,2,3,1,0:T(2,128)}, u32[]{:S(2)}) copy-start(f32[1,50,2,3,1536]{4,2,3,1,0:T(2,128)} %param.16) | copy-start | bytes 5529604
  3.2 1.0 %copy-start.1 = (bf16[1,2,3,1536,24]{3,4,2,1,0:T(8,128)(2,1)S(1)}, bf16[1,2,3,1536,24]{3,4,2,1,0:T(8,128)(2,1)}, u32[]{:S(2)}) copy-start(bf16[1,2,3,1536,24]{3,4,2,1,0:T(8,128)(2,1)} %param.17) | copy-start | bytes 1327108
  4.2 0.9 copy-start.2
  5.1 0.9 copy-start.3
  6.0 0.9 copy-start.4
  6.9 0.7 copy-start.5
  7.6 0.7 copy-start.6
  8.3 0.7 copy-start.7

commit v2 on v1

v2 whole, which is shorter than its diff:
```python
import math

import jax
import jax.numpy as jnp
from jax import lax
from jax.experimental import pallas as pl
from jax.experimental.pallas import tpu as pltpu
from jax.sharding import PartitionSpec as P

HEAD_DIM = 128
F32, BF16 = jnp.float32, jnp.bfloat16
MESH = pl.DeviceIdType.MESH
FACTOR = 1.0 / math.sqrt(HEAD_DIM)


def kernel(
    timestep, text_len, latent, text, prev_v, prev_t, blend_hbm, mod_hbm, gains_hbm, wqkv, wout,
    vout, tout,
    latent_v, text_v, old_v, old_t, blend, mod_all, gains, mod, turned,
    vsend, pack32, tsend, zv, zt, tokv, tokt, wq, packed,
    b, kv, qraw, qtraw, qall, kn, vall,
    osend, ssend, orecv, srecv, otrecv, strecv,
    wo, att, tall, tpk, pout, precv,
    send, r_z, r_w, r_y, r_q, r_qt, r_kv, r_qx, r_o, r_ot,
    r_wo, r_wox, r_att, r_attt, r_out, loc,
):
    c = lax.axis_index("comp")
    s = lax.axis_index("seq")
    odd = c % 2
    z, a0, a1 = s // 16, (s // 4) % 4, s % 4
    y = a0 + odd * (a1 - a0)
    x = a1 + odd * (a0 - a1)
    diag = y == x

    def at_seq(zz, yy, xx):
        return (c, zz * 16 + yy * (4 - 3 * odd) + xx * (1 + 3 * odd))

    def ypeer(d):
        return at_seq(z, (y + d) % 4, x)

    def zypeer(dz, dy):
        return at_seq((z + dz) % 4, (y + dy) % 4, x)

    def xpeer(d):
        return at_seq(z, y, (x + d) % 4)

    used = [0]
    always, on_diag, off_diag = [], [], []

    def copy_to(src, dst, recv, device, group=None):
        op = pltpu.make_async_remote_copy(
            src_ref=src, dst_ref=dst, send_sem=send.at[used[0]], recv_sem=recv,
            device_id=device, device_id_type=MESH,
        )
        used[0] += 1
        op.start()
        (always if group is None else group).append(op)

    def arrived(dst, recv):
        pltpu.make_async_remote_copy(
            src_ref=dst, dst_ref=dst, send_sem=send.at[0], recv_sem=recv,
            device_id=xpeer(1), device_id_type=MESH,
        ).wait_recv()

    nextc, prevc = (c + 1) % 4, (c + 3) % 4
    barrier = pltpu.get_barrier_semaphore()
    for d in range(4):
        pl.semaphore_signal(barrier, inc=1, device_id=(prevc, (s + 16 * d) % 64), device_id_type=MESH)
    for dz in range(4):
        for dy in range(4):
            if dz or dy:
                pl.semaphore_signal(barrier, inc=1, device_id=zypeer(dz, dy), device_id_type=MESH)
    for d in (1, 2, 3):
        pl.semaphore_signal(barrier, inc=1, device_id=xpeer(d), device_id_type=MESH)

    loads = [
        pltpu.make_async_copy(a, bb, loc.at[i])
        for i, (a, bb) in enumerate(
            (
                (latent, latent_v), (prev_v, old_v), (text, text_v), (prev_t, old_t),
                (blend_hbm, blend), (mod_hbm, mod_all), (gains_hbm, gains), (wqkv, wq.at[x]),
            )
        )
    ]
    for op in loads:
        op.start()
    for op in loads[:7]:
        op.wait()

    step = timestep[0]
    lane = lax.broadcasted_iota(jnp.int32, (2, 50), 1)
    pair = jnp.sum(jnp.where(lane == step, blend[...], 0.0), axis=1, keepdims=True)
    last = c == 3
    old = old_v[...]
    mixed = (pair[0:1] * latent_v[...].astype(F32) + pair[1:2] * old.astype(F32)).astype(BF16)
    vsend[...] = jnp.where(last, mixed, old)
    words = jnp.where(last, text_v[...], old_t[...]).astype(F32)
    for j in range(4):
        pack32[4 * j : 4 * j + 4, :] = words[:, 384 * j : 384 * j + 384]
    tsend[...] = pack32[...].astype(BF16)
    tokt[4:8] = jnp.zeros((4, 16, 1536), BF16)
    for st in range(2):
        for k in range(3):
            mod[3 * st + k : 3 * st + k + 1, :] = mod_all[step, k, st : st + 1, :]
        for k in range(2):
            turned[2 * st + k] = jnp.broadcast_to(gains[st, k : k + 1, :], (128, 128)).T

    pl.semaphore_wait(barrier, 22)

    for d in (0, 1, 3, 2):
        copy_to(vsend, zv.at[z], r_z.at[d, 0], (nextc, (s + 16 * d) % 64))
    for d in (0, 1, 3, 2):
        copy_to(tsend, zt.at[z], r_z.at[d, 1], (nextc, (s + 16 * d) % 64))
    for i, part in enumerate((pl.ds(0, 80), pl.ds(80, 64))):
        for d in (1, 3, 2):
            copy_to(wqkv.at[part], wq.at[x, part], r_w.at[d - 1, i], xpeer(d))

    def normed(wide, stream):
        center = wide - jnp.mean(wide, axis=-1, keepdims=True)
        spread = jnp.mean(center * center, axis=-1, keepdims=True)
        shift = mod[3 * stream : 3 * stream + 1, :]
        scale = mod[3 * stream + 1 : 3 * stream + 2, :]
        return (center * lax.rsqrt(spread + 1e-06) * (1.0 + scale) + shift).astype(BF16)

    def unpack(packed):
        return jnp.concatenate([packed[4 * j : 4 * j + 4, :] for j in range(4)], axis=1)

    for d in (0, 1, 3, 2):
        zz = (z + 4 - d) % 4
        arrived(zv.at[zz], r_z.at[d, 0])
        slot = y * 4 + zz
        tokv[slot] = normed(zv[zz].astype(F32), 0)
        for e in (1, 3, 2):
            copy_to(tokv.at[slot], tokv.at[slot], r_y.at[e - 1, d], ypeer(e))
    for d in (0, 1, 3, 2):
        arrived(zt.at[(z + 4 - d) % 4], r_z.at[d, 1])
    rows = jnp.concatenate([unpack(zt[j].astype(F32)) for j in range(4)], axis=0)
    tokt[y] = normed(rows, 1)
    for e in (1, 3, 2):
        copy_to(tokt.at[y], tokt.at[y], r_y.at[e - 1, 4], ypeer(e))

    def wo_part(d):
        return wout.at[:, pl.ds(pl.multiple_of(((z + d) % 4) * 384, 128), 384)]

    for d in (1, 3, 2):
        copy_to(wo_part(d), wo.at[x, y], r_wo.at[y], at_seq((z + d) % 4, z, x))
    wo_slot = used[0]
    used[0] += 1

    def wo_near():
        return pltpu.make_async_remote_copy(
            src_ref=wo_part(0), dst_ref=wo.at[x, y], send_sem=send.at[wo_slot],
            recv_sem=r_wo.at[y], device_id=at_seq(z, z, x), device_id_type=MESH,
        )

    def wo_own():
        return pltpu.make_async_copy(wo_part(0), wo.at[x, y], loc.at[8])

    @pl.when(y == z)
    def _():
        wo_own().start()

    @pl.when(y != z)
    def _():
        wo_near().start()

    loads[7].wait()

    def regroup(stream):
        wide = [wq[xx, 72 * stream : 72 * stream + 72].astype(F32) for xx in range(4)]
        packed[stream] = jnp.concatenate(
            [wide[xx][24 * j : 24 * j + 24] for j in range(3) for xx in range(4)], axis=0
        ).astype(BF16)

    def project(tokens, stream):
        return lax.dot_general(
            packed[stream], tokens, (((1,), (1,)), ((), ())), preferred_element_type=F32
        ).astype(BF16)

    for d in (1, 3, 2):
        arrived(wq.at[(x + 4 - d) % 4, pl.ds(0, 80)], r_w.at[d - 1, 0])
    regroup(0)
    order = (0, 1, 3, 2)
    for k, d in enumerate(order):
        yy = (y + 4 - d) % 4
        if d:
            for dz in range(4):
                arrived(tokv.at[yy * 4 + dz], r_y.at[d - 1, dz])
        b[k] = project(tokv[pl.ds(yy * 4, 4)].reshape(128, 1536), 0)
        if d:
            copy_to(b.at[k, 0:96], qraw.at[y], r_q.at[d - 1], ypeer(4 - d))
        else:
            qraw[y] = b[k, 0:96]
    for k, d in enumerate(order):
        yy = (y + 4 - d) % 4
        for e in (1, 3, 2):
            copy_to(b.at[k, 96:288], kv.at[yy, y], r_kv.at[e - 1, yy], ypeer(e))
        kv[yy, y] = b[k, 96:288]
    for d in (1, 3, 2):
        arrived(wq.at[(x + 4 - d) % 4, pl.ds(80, 64)], r_w.at[d - 1, 1])
    regroup(1)
    for e in (1, 3, 2):
        arrived(tokt.at[(y + 4 - e) % 4], r_y.at[e - 1, 4])
    b[4] = project(tokt[...].reshape(128, 1536), 1)
    to_diag = (y + 4 - x) % 4
    used_qt = used[0]
    used[0] += 1

    def text_query():
        return pltpu.make_async_remote_copy(
            src_ref=b.at[4, 0:96], dst_ref=qtraw.at[y], send_sem=send.at[used_qt],
            recv_sem=r_qt.at[to_diag - 1], device_id=at_seq(z, x, x), device_id_type=MESH,
        )

    @pl.when(diag)
    def _():
        qtraw[y] = b[4, 0:96]

    @pl.when(jnp.logical_not(diag))
    def _():
        text_query().start()

    for e in (1, 3, 2):
        copy_to(b.at[4, 96:288], kv.at[4, y], r_kv.at[e - 1, 4], ypeer(e))
    kv[4, y] = b[4, 96:288]

    def natural(groups):
        straight = [groups[g] for g in range(16)]
        crossed = [groups[(g % 4) * 4 + g // 4] for g in range(16)]
        return jnp.where(
            odd == 1, jnp.concatenate(crossed, axis=0), jnp.concatenate(straight, axis=0)
        )

    def by_rows(slabs):
        wide = [slabs[yy].astype(F32) for yy in range(4)]
        return natural([wide[g // 4][24 * (g % 4) : 24 * (g % 4) + 24] for g in range(16)])

    def head_norm(raw, gain):
        square = jnp.mean(raw * raw, axis=0, keepdims=True)
        return raw * lax.rsqrt(square + 1e-06) * gain

    gq_v, gk_v, gq_t, gk_t = [turned[j] for j in range(4)]

    def queries(raw, gain):
        return jnp.concatenate(
            [head_norm(raw[128 * h : 128 * h + 128], gain) for h in range(3)], axis=0
        ).astype(BF16)

    for d in (1, 3, 2):
        arrived(qraw.at[(y + d) % 4], r_q.at[d - 1])
    qall[x] = queries(by_rows(qraw), gq_v)
    for d in (1, 3, 2):
        copy_to(qall.at[x], qall.at[x], r_qx.at[d - 1, 0], xpeer(d))
    qt_first = used[0]
    used[0] += 3

    def text_queries(d):
        return pltpu.make_async_remote_copy(
            src_ref=qall.at[4], dst_ref=qall.at[4], send_sem=send.at[qt_first + d - 1],
            recv_sem=r_qx.at[0, 1], device_id=xpeer(d), device_id_type=MESH,
        )

    @pl.when(diag)
    def _():
        for d in (1, 3, 2):
            arrived(qtraw.at[(y + d) % 4], r_qt.at[d - 1])
        qall[4] = queries(by_rows(qtraw), gq_t)
        for d in (1, 3, 2):
            text_queries(d).start()

    for ch in range(5):
        for e in (1, 3, 2):
            arrived(kv.at[ch, 0], r_kv.at[e - 1, ch])
        keys = by_rows([kv[ch, yy, 0:96] for yy in range(4)])
        values = by_rows([kv[ch, yy, 96:192] for yy in range(4)])
        vall[:, 128 * ch : 128 * ch + 128] = values.astype(BF16)
        for h in range(3):
            key = head_norm(keys[128 * h : 128 * h + 128], gk_v if ch < 4 else gk_t).T
            kn[h, 128 * ch : 128 * ch + 128, :] = key.astype(BF16)
    @pl.when(y == z)
    def _():
        wo_own().wait()

    @pl.when(y != z)
    def _():
        arrived(wo.at[x, y], r_wo.at[y])

    for d in (1, 2, 3):
        arrived(wo.at[x, (y + d) % 4], r_wo.at[(y + d) % 4])

    for d in (1, 3, 2):
        copy_to(wo.at[x], wo.at[x], r_wox.at[d - 1], xpeer(d))

    for d in (1, 3, 2):
        arrived(qall.at[(x + 4 - d) % 4], r_qx.at[d - 1, 0])

    @pl.when(jnp.logical_not(diag))
    def _():
        arrived(qall.at[4], r_qx.at[0, 1])

    r = lax.broadcasted_iota(jnp.int32, (128, 128), 0)
    place = (r // 16) * (4 - 3 * odd) + x * (1 + 3 * odd)
    index = (((r % 16) // 4) * 16 + place) * 4 + r % 4
    usable = (r < 64) & (index < text_len[c])

    def attend(qc, h):
        scores = (
            jnp.dot(kn[h], qall[qc, 128 * h : 128 * h + 128, :], preferred_element_type=F32)
            * FACTOR
        )
        words = jnp.where(usable, scores[512:640], -1e30)
        scores = jnp.concatenate([scores[0:512], words], axis=0)
        highest = jnp.max(scores, axis=0, keepdims=True)
        weights = jnp.exp(scores - highest)
        total = jnp.sum(weights, axis=0, keepdims=True)
        out = jnp.dot(
            vall[128 * h : 128 * h + 128, :], weights.astype(BF16), preferred_element_type=F32
        )
        osend[h, qc] = (out / total).astype(BF16)
        ssend[h, qc, 0:1, :] = highest
        ssend[h, qc, 1:2, :] = total

    ot_first = used[0]
    used[0] += 6
    at_first = used[0]
    used[0] += 9

    def text_out(h, i):
        a, bb = ((osend, otrecv), (ssend, strecv))[i]
        return pltpu.make_async_remote_copy(
            src_ref=a.at[h, 4], dst_ref=bb.at[h, x], send_sem=send.at[ot_first + 2 * h + i],
            recv_sem=r_ot.at[(x + 4 - y) % 4 - 1, h, i], device_id=at_seq(z, y, y),
            device_id_type=MESH,
        )

    def text_att(h, d):
        part = att.at[4, pl.ds(128 * h, 128)]
        return pltpu.make_async_remote_copy(
            src_ref=part, dst_ref=part, send_sem=send.at[at_first + 3 * h + d - 1],
            recv_sem=r_attt.at[h], device_id=ypeer(d), device_id_type=MESH,
        )

    def attend_head(h):
        for d in (2, 1, 3):
            qc = (x + d) % 4
            attend(qc, h)
            copy_to(osend.at[h, qc], orecv.at[h, x], r_o.at[d - 1, h, 0], xpeer(d))
            copy_to(ssend.at[h, qc], srecv.at[h, x], r_o.at[d - 1, h, 1], xpeer(d))
        attend(4, h)

        @pl.when(diag)
        def _():
            otrecv[h, x] = osend[h, 4]
            strecv[h, x] = ssend[h, 4]

        @pl.when(jnp.logical_not(diag))
        def _():
            text_out(h, 0).start()
            text_out(h, 1).start()

        attend(x, h)
        orecv[h, x] = osend[h, x]
        srecv[h, x] = ssend[h, x]

    def combine(o, st, h):
        top = [st[h, i, 0:1, :] for i in range(4)]
        highest = jnp.maximum(jnp.maximum(top[0], top[1]), jnp.maximum(top[2], top[3]))
        share = [st[h, i, 1:2, :] * jnp.exp(top[i] - highest) for i in range(4)]
        total = share[0] + share[1] + share[2] + share[3]
        acc = jnp.zeros((128, 128), F32)
        for i in range(4):
            acc += (share[i] / total) * o[h, i].astype(F32)
        return acc.astype(BF16)

    def combine_head(h):
        part = pl.ds(128 * h, 128)
        for d in (1, 3, 2):
            arrived(orecv.at[h, x], r_o.at[d - 1, h, 0])
            arrived(srecv.at[h, x], r_o.at[d - 1, h, 1])
        att[y, part] = combine(orecv, srecv, h)
        for d in (1, 3, 2):
            copy_to(att.at[y, part], att.at[y, part], r_att.at[d - 1, h], ypeer(d))

        @pl.when(diag)
        def _():
            for d in (1, 3, 2):
                arrived(otrecv.at[h, x], r_ot.at[d - 1, h, 0])
                arrived(strecv.at[h, x], r_ot.at[d - 1, h, 1])
            att[4, part] = combine(otrecv, strecv, h)
            for d in (1, 3, 2):
                text_att(h, d).start()

    attend_head(0)
    attend_head(1)
    combine_head(0)
    attend_head(2)
    combine_head(1)
    combine_head(2)
    for d in (1, 3, 2):
        arrived(wo.at[x], r_wox.at[d - 1])
    weights_out = wo[...].reshape(768, 384)

    def project_out(values, stream):
        out = jnp.dot(weights_out, values, preferred_element_type=F32)
        return natural(
            [
                out[(xx * 4 + yy) * 48 + stream * 24 :][:24]
                for yy in range(4)
                for xx in range(4)
            ]
        ).T

    def video_block(slot):
        block = project_out(att[slot], 0).astype(BF16)
        for q in range(4):
            for j in range(3):
                pout[slot, q, 32 * j : 32 * j + 32, :] = block[
                    32 * q : 32 * q + 32, 128 * j : 128 * j + 128
                ]

    video_block(y)

    @pl.when(jnp.logical_not(diag))
    def _():
        for h in range(3):
            arrived(att.at[4, pl.ds(128 * h, 128)], r_attt.at[h])

    tall[...] = project_out(att[4], 1)
    for yy in range(4):
        for q in range(4):
            for j in range(3):
                pack32[4 * j : 4 * j + 4, 0:128] = tall[
                    16 * yy + 4 * q : 16 * yy + 4 * q + 4, 128 * j : 128 * j + 128
                ]
            tpk[yy, q] = pack32[:, 0:128].astype(BF16)

    for dy in (0, 1, 3, 2):
        slot = (y + dy) % 4
        if dy:
            for h in range(3):
                arrived(att.at[slot, pl.ds(128 * h, 128)], r_att.at[3 - dy, h])
            video_block(slot)
        for q in range(4):
            pout[slot, q, 96:112, :] = tpk[slot, q]
        for dz in (2, 1, 3, 0):
            if dy or dz:
                copy_to(
                    pout.at[slot, (z + dz) % 4], precv.at[z, y], r_out.at[dz, dy], zypeer(dz, dy)
                )
            else:
                precv[z, y] = pout[slot, z]

    for dy in (0, 1, 3, 2):
        for dz in (0, 1, 3, 2):
            if dy or dz:
                arrived(precv.at[z, y], r_out.at[dz, dy])
    for yy in range(4):
        total = precv[0, yy].astype(F32)
        for zz in range(1, 4):
            total += precv[zz, yy].astype(F32)
        total = total.astype(BF16).astype(F32)
        for j in range(3):
            at = pl.ds(384 * yy + 128 * j, 128)
            vout[:, at] = (
                zv[z, :, at].astype(F32) + mod[2:3, at] * total[32 * j : 32 * j + 32]
            ).astype(BF16)
            own = zt[z, 4 * yy : 4 * yy + 4, 128 * j : 128 * j + 128].astype(F32)
            tout[:, at] = (own + mod[5:6, at] * total[96 + 4 * j : 100 + 4 * j]).astype(BF16)

    for op in always:
        op.wait_send()

    @pl.when(y != z)
    def _():
        wo_near().wait_send()

    @pl.when(diag)
    def _():
        for d in (1, 3, 2):
            text_queries(d).wait_send()
            for h in range(3):
                text_att(h, d).wait_send()

    @pl.when(jnp.logical_not(diag))
    def _():
        text_query().wait_send()
        for h in range(3):
            text_out(h, 0).wait_send()
            text_out(h, 1).wait_send()


def body(
    latent_video, text_embed, previous_video, previous_text, noise_blend, modulation,
    w_qkv, w_out, qk_gain, text_len, timestep,
):
    blend = noise_blend.T
    mod = modulation[0].transpose(0, 2, 1, 3)
    gains = qk_gain[0]
    wqkv = w_qkv[0].transpose(0, 1, 3, 2).reshape(144, 1536)
    wout = w_out[0].transpose(0, 2, 1).reshape(48, 1536)
    vm = pl.BlockSpec(memory_space=pltpu.VMEM)
    sm = pl.BlockSpec(memory_space=pltpu.SMEM)
    hbm = pl.BlockSpec(memory_space=pltpu.HBM)

    def buf(*shape, dtype=BF16):
        return pltpu.VMEM(shape, dtype)

    def sems(*shape):
        return pltpu.SemaphoreType.DMA(shape)

    video, words = pl.pallas_call(
        kernel,
        out_shape=(
            jax.ShapeDtypeStruct((32, 1536), BF16),
            jax.ShapeDtypeStruct((4, 1536), BF16),
        ),
        in_specs=[sm, sm] + [hbm] * 9,
        out_specs=(vm, vm),
        scratch_shapes=[
            buf(32, 1536), buf(4, 1536), buf(32, 1536), buf(4, 1536), buf(2, 50, dtype=F32),
            buf(50, 3, 2, 1536, dtype=F32), buf(2, 2, 128, dtype=F32), buf(8, 1536, dtype=F32),
            buf(4, 128, 128, dtype=F32),
            buf(32, 1536), buf(16, 384, dtype=F32), buf(16, 384),
            buf(4, 32, 1536), buf(4, 16, 384), buf(16, 32, 1536), buf(8, 16, 1536),
            buf(4, 144, 1536), buf(2, 288, 1536),
            buf(5, 288, 128), buf(5, 4, 192, 128), buf(4, 96, 128), buf(4, 96, 128),
            buf(5, 384, 128), buf(3, 640, 128), buf(384, 640),
            buf(3, 5, 128, 128), buf(3, 5, 8, 128, dtype=F32),
            buf(3, 4, 128, 128), buf(3, 4, 8, 128, dtype=F32),
            buf(3, 4, 128, 128), buf(3, 4, 8, 128, dtype=F32),
            buf(4, 4, 48, 384), buf(5, 384, 128), buf(128, 384, dtype=F32), buf(4, 4, 16, 128),
            buf(4, 4, 112, 128), buf(4, 4, 112, 128),
            sems(144), sems(4, 2), sems(3, 2), sems(3, 5), sems(3), sems(3), sems(3, 5),
            sems(3, 2), sems(3, 3, 2), sems(3, 3, 2), sems(4), sems(3), sems(3, 3), sems(3),
            sems(4, 4), sems(9),
        ],
        compiler_params=pltpu.CompilerParams(
            collective_id=0, has_side_effects=True, vmem_limit_bytes=62 << 20
        ),
    )(
        timestep, text_len, latent_video, text_embed, previous_video[0], previous_text[0],
        blend, mod, gains, wqkv, wout,
    )
    return video[None], words[None]


def solution(mesh):
    placed = (
        P("seq", None),
        P("seq", None),
        P("comp", "seq", None),
        P("comp", "seq", None),
        P(),
        P("comp", None, None, None, None),
        P("comp", None, None, None, "seq"),
        P("comp", None, None, "seq"),
        P("comp", None, None, None),
        P(),
        P(),
    )
    return jax.shard_map(
        body,
        mesh=mesh,
        in_specs=placed,
        out_specs=(P("comp", "seq", None), P("comp", "seq", None)),
        check_vma=False,
    )
```

time: 93.6 us -> 84 us (0.90)
  the two profiles are of different devices: /device:TPU:16 before, /device:TPU:1 now
where the time goes in v2:
time: 84 us; the launch traced here: 83.7 us
  Pallas kernels  79.6 us (95%)
  local copies, waits for them, and re-layouts  2.85 us (3%)
  between operations  1.29 us (2%)
    pallas_call x1, Pallas kernels, body(): pl.pallas_call(kernel, out_shape=(jax.ShapeDtypeStruct((32, 1536), BF16),...  79.6 us
    unnamed x2, local copies, waits for them, and re-layouts  2.85 us

profile of v2, /device:TPU:1, one launch (start us, length us, event | category | flops | bytes accessed | tf_op | source)
XLA Modules:
  0.0 83.7 jit_solution(757391038441299693)
XLA Ops:
  1.3 79.6 %shard_map.122 = (bf16[32,1536]{1,0:T(8,128)(2,1)}, bf16[4,1536]{1,0:T(4,128)(2,1)}) custom-call(s32[1]{0:T(128)S(6)} %copy.15.timestep, s32[4]{0:T(128)} %text_len.1, bf16[32,1536]{1,0:T(8,128)(2,1)} %latent.1, bf16[4,1536]{1,0:T(4,128)(2,1)} %text.1, bf16[32,1536]{1,0:T(8,128)(2,1)} %bitcast.23, bf16[4,1536]{1,0:T(4,128)(2,1)} %bitcast.25, ...), custom_call_target="tpu_custom_call" | custom-call | tf_op jit(solution)/shard_map/pallas_call | solution.py:511
  80.9 1.5 %copy.16 = bf16[1,32,1536]{2,1,0:T(8,128)(2,1)} copy(bf16[1,32,1536]{2,1,0:T(8,128)(2,1)} %bitcast.22) | data formatting | bytes 196608
  82.4 1.3 %copy.17 = bf16[1,4,1536]{2,1,0:T(4,128)(2,1)} copy(bf16[1,4,1536]{2,1,0:T(4,128)(2,1)} %bitcast.24) | data formatting | bytes 24576

commit v3 on v2

--- a/solution.py
+++ b/solution.py
@@ -84,7 +84,7 @@
     ]
     for op in loads:
         op.start()
-    for op in loads[:7]:
+    for op in loads[:5]:
         op.wait()
 
     step = timestep[0]
@@ -99,21 +99,23 @@
         pack32[4 * j : 4 * j + 4, :] = words[:, 384 * j : 384 * j + 384]
     tsend[...] = pack32[...].astype(BF16)
     tokt[4:8] = jnp.zeros((4, 16, 1536), BF16)
+    pl.semaphore_wait(barrier, 22)
+
+    for d in (2, 1, 3, 0):
+        copy_to(tsend, zt.at[z], r_z.at[d, 1], (nextc, (s + 16 * d) % 64))
+    for d in (0, 1, 3, 2):
+        copy_to(vsend, zv.at[z], r_z.at[d, 0], (nextc, (s + 16 * d) % 64))
+    for i, part in enumerate((pl.ds(0, 80), pl.ds(80, 64))):
+        for d in (1, 3, 2):
+            copy_to(wqkv.at[part], wq.at[x, part], r_w.at[d - 1, i], xpeer(d))
+
+    for op in loads[5:7]:
+        op.wait()
     for st in range(2):
         for k in range(3):
             mod[3 * st + k : 3 * st + k + 1, :] = mod_all[step, k, st : st + 1, :]
         for k in range(2):
             turned[2 * st + k] = jnp.broadcast_to(gains[st, k : k + 1, :], (128, 128)).T
-
-    pl.semaphore_wait(barrier, 22)
-
-    for d in (0, 1, 3, 2):
-        copy_to(vsend, zv.at[z], r_z.at[d, 0], (nextc, (s + 16 * d) % 64))
-    for d in (0, 1, 3, 2):
-        copy_to(tsend, zt.at[z], r_z.at[d, 1], (nextc, (s + 16 * d) % 64))
-    for i, part in enumerate((pl.ds(0, 80), pl.ds(80, 64))):
-        for d in (1, 3, 2):
-            copy_to(wqkv.at[part], wq.at[x, part], r_w.at[d - 1, i], xpeer(d))
 
     def normed(wide, stream):
         center = wide - jnp.mean(wide, axis=-1, keepdims=True)
@@ -125,44 +127,23 @@
     def unpack(packed):
         return jnp.concatenate([packed[4 * j : 4 * j + 4, :] for j in range(4)], axis=1)
 
-    for d in (0, 1, 3, 2):
+    def norm_piece(d):
         zz = (z + 4 - d) % 4
         arrived(zv.at[zz], r_z.at[d, 0])
-        slot = y * 4 + zz
+        slot = zz * 4 + y
         tokv[slot] = normed(zv[zz].astype(F32), 0)
         for e in (1, 3, 2):
             copy_to(tokv.at[slot], tokv.at[slot], r_y.at[e - 1, d], ypeer(e))
+
+    norm_piece(0)
     for d in (0, 1, 3, 2):
         arrived(zt.at[(z + 4 - d) % 4], r_z.at[d, 1])
     rows = jnp.concatenate([unpack(zt[j].astype(F32)) for j in range(4)], axis=0)
     tokt[y] = normed(rows, 1)
     for e in (1, 3, 2):
         copy_to(tokt.at[y], tokt.at[y], r_y.at[e - 1, 4], ypeer(e))
-
-    def wo_part(d):
-        return wout.at[:, pl.ds(pl.multiple_of(((z + d) % 4) * 384, 128), 384)]
-
-    for d in (1, 3, 2):
-        copy_to(wo_part(d), wo.at[x, y], r_wo.at[y], at_seq((z + d) % 4, z, x))
-    wo_slot = used[0]
-    used[0] += 1
-
-    def wo_near():
-        return pltpu.make_async_remote_copy(
-            src_ref=wo_part(0), dst_ref=wo.at[x, y], send_sem=send.at[wo_slot],
-            recv_sem=r_wo.at[y], device_id=at_seq(z, z, x), device_id_type=MESH,
-        )
-
-    def wo_own():
-        return pltpu.make_async_copy(wo_part(0), wo.at[x, y], loc.at[8])
-
-    @pl.when(y == z)
-    def _():
-        wo_own().start()
-
-    @pl.when(y != z)
-    def _():
-        wo_near().start()
+    norm_piece(1)
+    norm_piece(3)
 
     loads[7].wait()
 
@@ -177,25 +158,100 @@
             packed[stream], tokens, (((1,), (1,)), ((), ())), preferred_element_type=F32
         ).astype(BF16)
 
+    def natural(groups):
+        straight = [groups[g] for g in range(16)]
+        crossed = [groups[(g % 4) * 4 + g // 4] for g in range(16)]
+        return jnp.where(
+            odd == 1, jnp.concatenate(crossed, axis=0), jnp.concatenate(straight, axis=0)
+        )
+
+    def by_rows(slabs):
+        wide = [slabs[yy].astype(F32) for yy in range(4)]
+        return natural([wide[g // 4][24 * (g % 4) : 24 * (g % 4) + 24] for g in range(16)])
+
+    def head_norm(raw, gain):
+        square = jnp.mean(raw * raw, axis=0, keepdims=True)
+        return raw * lax.rsqrt(square + 1e-06) * gain
+
+    gq_v, gk_v, gq_t, gk_t = [turned[j] for j in range(4)]
+
+    def queries(raw, gain):
+        return jnp.concatenate(
+            [head_norm(raw[128 * h : 128 * h + 128], gain) for h in range(3)], axis=0
+        ).astype(BF16)
+
+    def set_keys(ch):
+        for e in (1, 3, 2):
+            arrived(kv.at[ch, 0], r_kv.at[e - 1, ch])
+        keys = by_rows([kv[ch, yy, 0:96] for yy in range(4)])
+        values = by_rows([kv[ch, yy, 96:192] for yy in range(4)])
+        vall[:, 128 * ch : 128 * ch + 128] = values.astype(BF16)
+        for h in range(3):
+            key = head_norm(keys[128 * h : 128 * h + 128], gk_v if ch < 4 else gk_t)
+            kn[h, 128 * ch : 128 * ch + 128, :] = key.astype(BF16).T
+
+    query_first = used[0]
+    used[0] += 4
+
+    def query_send(k, zz):
+        return pltpu.make_async_remote_copy(
+            src_ref=b.at[k, 0:96], dst_ref=qraw.at[y], send_sem=send.at[query_first + k],
+            recv_sem=r_q.at[y], device_id=at_seq(z, zz, x), device_id_type=MESH,
+        )
+
+    order = (0, 1, 3, 2)
+
+    def video_chunk(k):
+        d = order[k]
+        zz = (z + 4 - d) % 4
+        for e in (1, 3, 2):
+            arrived(tokv.at[zz * 4 + (y + 4 - e) % 4], r_y.at[e - 1, d])
+        b[k] = project(tokv[pl.ds(zz * 4, 4)].reshape(128, 1536), 0)
+
+        @pl.when(zz == y)
+        def _():
+            qraw[y] = b[k, 0:96]
+
+        @pl.when(zz != y)
+        def _():
+            query_send(k, zz).start()
+
+        for e in (1, 3, 2):
+            copy_to(b.at[k, 96:288], kv.at[k, y], r_kv.at[e - 1, k], ypeer(e))
+        kv[k, y] = b[k, 96:288]
+
     for d in (1, 3, 2):
         arrived(wq.at[(x + 4 - d) % 4, pl.ds(0, 80)], r_w.at[d - 1, 0])
     regroup(0)
-    order = (0, 1, 3, 2)
-    for k, d in enumerate(order):
-        yy = (y + 4 - d) % 4
-        if d:
-            for dz in range(4):
-                arrived(tokv.at[yy * 4 + dz], r_y.at[d - 1, dz])
-        b[k] = project(tokv[pl.ds(yy * 4, 4)].reshape(128, 1536), 0)
-        if d:
-            copy_to(b.at[k, 0:96], qraw.at[y], r_q.at[d - 1], ypeer(4 - d))
-        else:
-            qraw[y] = b[k, 0:96]
-    for k, d in enumerate(order):
-        yy = (y + 4 - d) % 4
-        for e in (1, 3, 2):
-            copy_to(b.at[k, 96:288], kv.at[yy, y], r_kv.at[e - 1, yy], ypeer(e))
-        kv[yy, y] = b[k, 96:288]
+    video_chunk(0)
+    norm_piece(2)
+    def wo_part(d):
+        return wout.at[:, pl.ds(pl.multiple_of(((z + d) % 4) * 384, 128), 384)]
+
+    for d in (1, 3, 2):
+        copy_to(wo_part(d), wo.at[x, y], r_wo.at[y], at_seq((z + d) % 4, z, x))
+    wo_slot = used[0]
+    used[0] += 1
+
+    def wo_near():
+        return pltpu.make_async_remote_copy(
+            src_ref=wo_part(0), dst_ref=wo.at[x, y], send_sem=send.at[wo_slot],
+            recv_sem=r_wo.at[y], device_id=at_seq(z, z, x), device_id_type=MESH,
+        )
+
+    def wo_own():
+        return pltpu.make_async_copy(wo_part(0), wo.at[x, y], loc.at[8])
+
+    @pl.when(y == z)
+    def _():
+        wo_own().start()
+
+    @pl.when(y != z)
+    def _():
+        wo_near().start()
+
+    video_chunk(1)
+    video_chunk(2)
     for d in (1, 3, 2):
         arrived(wq.at[(x + 4 - d) % 4, pl.ds(80, 64)], r_w.at[d - 1, 1])
     regroup(1)
@@ -224,30 +280,10 @@
         copy_to(b.at[4, 96:288], kv.at[4, y], r_kv.at[e - 1, 4], ypeer(e))
     kv[4, y] = b[4, 96:288]
 
-    def natural(groups):
-        straight = [groups[g] for g in range(16)]
-        crossed = [groups[(g % 4) * 4 + g // 4] for g in range(16)]
-        return jnp.where(
-            odd == 1, jnp.concatenate(crossed, axis=0), jnp.concatenate(straight, axis=0)
-        )
-
-    def by_rows(slabs):
-        wide = [slabs[yy].astype(F32) for yy in range(4)]
-        return natural([wide[g // 4][24 * (g % 4) : 24 * (g % 4) + 24] for g in range(16)])
-
-    def head_norm(raw, gain):
-        square = jnp.mean(raw * raw, axis=0, keepdims=True)
-        return raw * lax.rsqrt(square + 1e-06) * gain
-
-    gq_v, gk_v, gq_t, gk_t = [turned[j] for j in range(4)]
-
-    def queries(raw, gain):
-        return jnp.concatenate(
-            [head_norm(raw[128 * h : 128 * h + 128], gain) for h in range(3)], axis=0
-        ).astype(BF16)
-
-    for d in (1, 3, 2):
-        arrived(qraw.at[(y + d) % 4], r_q.at[d - 1])
+    set_keys(0)
+    video_chunk(3)
+    for d in (1, 3, 2):
+        arrived(qraw.at[(y + d) % 4], r_q.at[(y + d) % 4])
     qall[x] = queries(by_rows(qraw), gq_v)
     for d in (1, 3, 2):
         copy_to(qall.at[x], qall.at[x], r_qx.at[d - 1, 0], xpeer(d))
@@ -268,15 +304,8 @@
         for d in (1, 3, 2):
             text_queries(d).start()
 
-    for ch in range(5):
-        for e in (1, 3, 2):
-            arrived(kv.at[ch, 0], r_kv.at[e - 1, ch])
-        keys = by_rows([kv[ch, yy, 0:96] for yy in range(4)])
-        values = by_rows([kv[ch, yy, 96:192] for yy in range(4)])
-        vall[:, 128 * ch : 128 * ch + 128] = values.astype(BF16)
-        for h in range(3):
-            key = head_norm(keys[128 * h : 128 * h + 128], gk_v if ch < 4 else gk_t).T
-            kn[h, 128 * ch : 128 * ch + 128, :] = key.astype(BF16)
+    for ch in (1, 2, 4, 3):
+        set_keys(ch)
     @pl.when(y == z)
     def _():
         wo_own().wait()
@@ -434,6 +463,15 @@
                 ]
             tpk[yy, q] = pack32[:, 0:128].astype(BF16)
 
+    own_first = used[0]
+    used[0] += 4
+
+    def own_row(dy, slot):
+        return pltpu.make_async_remote_copy(
+            src_ref=pout.at[slot, y], dst_ref=precv.at[z, y], send_sem=send.at[own_first + dy],
+            recv_sem=r_out.at[z, y], device_id=at_seq(slot, y, x), device_id_type=MESH,
+        )
+
     for dy in (0, 1, 3, 2):
         slot = (y + dy) % 4
         if dy:
@@ -441,19 +479,23 @@
                 arrived(att.at[slot, pl.ds(128 * h, 128)], r_att.at[3 - dy, h])
             video_block(slot)
         for q in range(4):
-            pout[slot, q, 96:112, :] = tpk[slot, q]
-        for dz in (2, 1, 3, 0):
-            if dy or dz:
-                copy_to(
-                    pout.at[slot, (z + dz) % 4], precv.at[z, y], r_out.at[dz, dy], zypeer(dz, dy)
-                )
-            else:
-                precv[z, y] = pout[slot, z]
+            pout[slot, q, 96:112, :] = tpk[q, slot]
+        for e in (2, 1, 3):
+            q = (y + e) % 4
+            copy_to(pout.at[slot, q], precv.at[z, y], r_out.at[z, y], at_seq(slot, q, x))
+
+        @pl.when(slot == z)
+        def _():
+            precv[z, y] = pout[slot, y]
+
+        @pl.when(slot != z)
+        def _():
+            own_row(dy, slot).start()
 
     for dy in (0, 1, 3, 2):
         for dz in (0, 1, 3, 2):
             if dy or dz:
-                arrived(precv.at[z, y], r_out.at[dz, dy])
+                arrived(precv.at[z, y], r_out.at[(z + dz) % 4, (y + dy) % 4])
     for yy in range(4):
         total = precv[0, yy].astype(F32)
         for zz in range(1, 4):
@@ -469,6 +511,15 @@
 
     for op in always:
         op.wait_send()
+
+    for k, d in enumerate(order):
+        @pl.when((z + 4 - d) % 4 != y)
+        def _():
+            query_send(k, (z + 4 - d) % 4).wait_send()
+
+        @pl.when((y + d) % 4 != z)
+        def _():
+            own_row(d, (y + d) % 4).wait_send()
 
     @pl.when(y != z)
     def _():
@@ -530,16 +581,22 @@
             buf(3, 4, 128, 128), buf(3, 4, 8, 128, dtype=F32),
             buf(4, 4, 48, 384), buf(5, 384, 128), buf(128, 384, dtype=F32), buf(4, 4, 16, 128),
             buf(4, 4, 112, 128), buf(4, 4, 112, 128),
-            sems(144), sems(4, 2), sems(3, 2), sems(3, 5), sems(3), sems(3), sems(3, 5),
+            sems(144), sems(4, 2), sems(3, 2), sems(3, 5), sems(4), sems(3), sems(3, 5),
             sems(3, 2), sems(3, 3, 2), sems(3, 3, 2), sems(4), sems(3), sems(3, 3), sems(3),
             sems(4, 4), sems(9),
         ],
         compiler_params=pltpu.CompilerParams(
-            collective_id=0, has_side_effects=True, vmem_limit_bytes=62 << 20
+            collective_id=0, has_side_effects=True, vmem_limit_bytes=48 << 20
         ),
     )(
-        timestep, text_len, latent_video, text_embed, previous_video[0], previous_text[0],
-        blend, mod, gains, wqkv, wout,
+        timestep, text_len,
+        *[
+            pltpu.with_memory_space_constraint(a, pltpu.HBM)
+            for a in (
+                latent_video, text_embed, previous_video[0], previous_text[0],
+                blend, mod, gains, wqkv, wout,
+            )
+        ],
     )
     return video[None], words[None]
 

time: 84 us -> 78.1 us (0.930)
  the two profiles are of different devices: /device:TPU:1 before, /device:TPU:2 now
where the time goes in v3:
time: 78.1 us; the launch traced here: 77 us
  Pallas kernels  73.8 us (94%)
  local copies, waits for them, and re-layouts  1.89 us (2%)
  between operations  1.3 us (2%)
    pallas_call x1, Pallas kernels, body(): pl.pallas_call(kernel, out_shape=(jax.ShapeDtypeStruct((32, 1536), BF16),...  73.8 us
    unnamed x4, local copies, waits for them, and re-layouts  1.89 us

profile of v3, /device:TPU:2, one launch (start us, length us, event | category | flops | bytes accessed | tf_op | source)
XLA Modules:
  0.0 77.0 jit_solution(7024595644627760664)
XLA Ops:
  1.3 0.0 copy-start
  1.3 0.6 copy-done
  1.9 73.8 %shard_map.122 = (bf16[32,1536]{1,0:T(8,128)(2,1)S(1)}, bf16[4,1536]{1,0:T(4,128)(2,1)S(1)}) custom-call(s32[1]{0:T(128)S(6)} %copy.15.timestep, s32[4]{0:T(128)S(1)} %copy-done, bf16[32,1536]{1,0:T(8,128)(2,1)} %latent.1, bf16[4,1536]{1,0:T(4,128)(2,1)} %text.1, bf16[32,1536]{1,0:T(8,128)(2,1)} %bitcast.24, bf16[4,1536]{1,0:T(4,128)(2,1)} %bitcast.25, ...), custom_call_target="tpu_custom_call" | custom-call | tf_op jit(solution)/shard_map/pallas_call | solution.py:562
  75.7 0.6 copy.16
  76.4 0.6 copy.17
Async XLA Ops:
  1.3 0.7 copy-start

commit v4 on v3

--- a/solution.py
+++ b/solution.py
@@ -20,7 +20,7 @@
     vsend, pack32, tsend, zv, zt, tokv, tokt, wq, packed,
     b, kv, qraw, qtraw, qall, kn, vall,
     osend, ssend, orecv, srecv, otrecv, strecv,
-    wo, att, tall, tpk, pout, precv,
+    wo, att, tall, own_words, pout, precv,
     send, r_z, r_w, r_y, r_q, r_qt, r_kv, r_qx, r_o, r_ot,
     r_wo, r_wox, r_att, r_attt, r_out, loc,
 ):
@@ -327,17 +327,18 @@
     def _():
         arrived(qall.at[4], r_qx.at[0, 1])
 
-    r = lax.broadcasted_iota(jnp.int32, (128, 128), 0)
+    r = lax.broadcasted_iota(jnp.int32, (128, 256), 0)
     place = (r // 16) * (4 - 3 * odd) + x * (1 + 3 * odd)
     index = (((r % 16) // 4) * 16 + place) * 4 + r % 4
     usable = (r < 64) & (index < text_len[c])
 
-    def attend(qc, h):
-        scores = (
-            jnp.dot(kn[h], qall[qc, 128 * h : 128 * h + 128, :], preferred_element_type=F32)
-            * FACTOR
-        )
-        words = jnp.where(usable, scores[512:640], -1e30)
+    def attend(slots, h):
+        wide = 128 * len(slots)
+        queries_in = jnp.concatenate(
+            [qall[slot, 128 * h : 128 * h + 128, :] for slot in slots], axis=1
+        )
+        scores = jnp.dot(kn[h], queries_in, preferred_element_type=F32) * FACTOR
+        words = jnp.where(usable[:, 0:wide], scores[512:640], -1e30)
         scores = jnp.concatenate([scores[0:512], words], axis=0)
         highest = jnp.max(scores, axis=0, keepdims=True)
         weights = jnp.exp(scores - highest)
@@ -345,9 +346,12 @@
         out = jnp.dot(
             vall[128 * h : 128 * h + 128, :], weights.astype(BF16), preferred_element_type=F32
         )
-        osend[h, qc] = (out / total).astype(BF16)
-        ssend[h, qc, 0:1, :] = highest
-        ssend[h, qc, 1:2, :] = total
+        out = (out / total).astype(BF16)
+        for i, slot in enumerate(slots):
+            part = slice(128 * i, 128 * i + 128)
+            osend[h, slot] = out[:, part]
+            ssend[h, slot, 0:1, :] = highest[:, part]
+            ssend[h, slot, 1:2, :] = total[:, part]
 
     ot_first = used[0]
     used[0] += 6
@@ -370,12 +374,16 @@
         )
 
     def attend_head(h):
-        for d in (2, 1, 3):
+        def send_part(d):
             qc = (x + d) % 4
-            attend(qc, h)
             copy_to(osend.at[h, qc], orecv.at[h, x], r_o.at[d - 1, h, 0], xpeer(d))
             copy_to(ssend.at[h, qc], srecv.at[h, x], r_o.at[d - 1, h, 1], xpeer(d))
-        attend(4, h)
+
+        attend(((x + 2) % 4, (x + 1) % 4), h)
+        send_part(2)
+        send_part(1)
+        attend(((x + 3) % 4, 4), h)
+        send_part(3)
 
         @pl.when(diag)
         def _():
@@ -387,7 +395,7 @@
             text_out(h, 0).start()
             text_out(h, 1).start()
 
-        attend(x, h)
+        attend((x,), h)
         orecv[h, x] = osend[h, x]
         srecv[h, x] = ssend[h, x]
 
@@ -449,6 +457,44 @@
 
     video_block(y)
 
+    own_first = used[0]
+    used[0] += 8
+    rows_of = (pl.ds(0, 96), pl.ds(96, 16))
+
+    def own_row(dy, i):
+        slot = (y + dy) % 4
+        return pltpu.make_async_remote_copy(
+            src_ref=pout.at[slot, y, rows_of[i]], dst_ref=precv.at[z, y, rows_of[i]],
+            send_sem=send.at[own_first + 2 * dy + i], recv_sem=r_out.at[z, y, i],
+            device_id=at_seq(slot, y, x), device_id_type=MESH,
+        )
+
+    def leave(dy, i):
+        slot = (y + dy) % 4
+        for e in (2, 1, 3):
+            q = (y + e) % 4
+            copy_to(
+                pout.at[slot, q, rows_of[i]], precv.at[z, y, rows_of[i]], r_out.at[z, y, i],
+                at_seq(slot, q, x),
+            )
+
+        @pl.when(slot == z)
+        def _():
+            precv[z, y, rows_of[i], :] = pout[slot, y, rows_of[i], :]
+
+        @pl.when(slot != z)
+        def _():
+            own_row(dy, i).start()
+
+    own_words[...] = unpack(zt[z].astype(F32))
+    leave(0, 0)
+    for dy in (1, 3, 2):
+        slot = (y + dy) % 4
+        for h in range(3):
+            arrived(att.at[slot, pl.ds(128 * h, 128)], r_att.at[3 - dy, h])
+        video_block(slot)
+        leave(dy, 0)
+
     @pl.when(jnp.logical_not(diag))
     def _():
         for h in range(3):
@@ -461,52 +507,27 @@
                 pack32[4 * j : 4 * j + 4, 0:128] = tall[
                     16 * yy + 4 * q : 16 * yy + 4 * q + 4, 128 * j : 128 * j + 128
                 ]
-            tpk[yy, q] = pack32[:, 0:128].astype(BF16)
-
-    own_first = used[0]
-    used[0] += 4
-
-    def own_row(dy, slot):
-        return pltpu.make_async_remote_copy(
-            src_ref=pout.at[slot, y], dst_ref=precv.at[z, y], send_sem=send.at[own_first + dy],
-            recv_sem=r_out.at[z, y], device_id=at_seq(slot, y, x), device_id_type=MESH,
-        )
+            pout[q, yy, 96:112, :] = pack32[:, 0:128].astype(BF16)
 
     for dy in (0, 1, 3, 2):
-        slot = (y + dy) % 4
-        if dy:
-            for h in range(3):
-                arrived(att.at[slot, pl.ds(128 * h, 128)], r_att.at[3 - dy, h])
-            video_block(slot)
-        for q in range(4):
-            pout[slot, q, 96:112, :] = tpk[q, slot]
-        for e in (2, 1, 3):
-            q = (y + e) % 4
-            copy_to(pout.at[slot, q], precv.at[z, y], r_out.at[z, y], at_seq(slot, q, x))
-
-        @pl.when(slot == z)
-        def _():
-            precv[z, y] = pout[slot, y]
-
-        @pl.when(slot != z)
-        def _():
-            own_row(dy, slot).start()
+        leave(dy, 1)
 
     for dy in (0, 1, 3, 2):
+        yy = (y + dy) % 4
         for dz in (0, 1, 3, 2):
             if dy or dz:
-                arrived(precv.at[z, y], r_out.at[(z + dz) % 4, (y + dy) % 4])
-    for yy in range(4):
+                for i in range(2):
+                    arrived(precv.at[z, y, rows_of[i]], r_out.at[(z + dz) % 4, yy, i])
         total = precv[0, yy].astype(F32)
         for zz in range(1, 4):
             total += precv[zz, yy].astype(F32)
         total = total.astype(BF16).astype(F32)
         for j in range(3):
-            at = pl.ds(384 * yy + 128 * j, 128)
+            at = pl.ds(pl.multiple_of(384 * yy + 128 * j, 128), 128)
             vout[:, at] = (
                 zv[z, :, at].astype(F32) + mod[2:3, at] * total[32 * j : 32 * j + 32]
             ).astype(BF16)
-            own = zt[z, 4 * yy : 4 * yy + 4, 128 * j : 128 * j + 128].astype(F32)
+            own = own_words[:, at]
             tout[:, at] = (own + mod[5:6, at] * total[96 + 4 * j : 100 + 4 * j]).astype(BF16)
 
     for op in always:
@@ -519,7 +540,8 @@
 
         @pl.when((y + d) % 4 != z)
         def _():
-            own_row(d, (y + d) % 4).wait_send()
+            for i in range(2):
+                own_row(d, i).wait_send()
 
     @pl.when(y != z)
     def _():
@@ -579,11 +601,11 @@
             buf(3, 5, 128, 128), buf(3, 5, 8, 128, dtype=F32),
             buf(3, 4, 128, 128), buf(3, 4, 8, 128, dtype=F32),
             buf(3, 4, 128, 128), buf(3, 4, 8, 128, dtype=F32),
-            buf(4, 4, 48, 384), buf(5, 384, 128), buf(128, 384, dtype=F32), buf(4, 4, 16, 128),
+            buf(4, 4, 48, 384), buf(5, 384, 128), buf(128, 384, dtype=F32), buf(4, 1536, dtype=F32),
             buf(4, 4, 112, 128), buf(4, 4, 112, 128),
-            sems(144), sems(4, 2), sems(3, 2), sems(3, 5), sems(4), sems(3), sems(3, 5),
+            sems(176), sems(4, 2), sems(3, 2), sems(3, 5), sems(4), sems(3), sems(3, 5),
             sems(3, 2), sems(3, 3, 2), sems(3, 3, 2), sems(4), sems(3), sems(3, 3), sems(3),
-            sems(4, 4), sems(9),
+            sems(4, 4, 2), sems(9),
         ],
         compiler_params=pltpu.CompilerParams(
             collective_id=0, has_side_effects=True, vmem_limit_bytes=48 << 20

time: 78.1 us -> 77.5 us (level); the launches traced: 77 us -> 77.4 us
  no operation moved by 1% of the time
where the time goes in v4:
time: 77.5 us; the launch traced here: 77.4 us
  Pallas kernels  74.2 us (96%)
  local copies, waits for them, and re-layouts  1.89 us (2%)
  between operations  1.3 us (2%)
    pallas_call x1, Pallas kernels, body(): pl.pallas_call(kernel, out_shape=(jax.ShapeDtypeStruct((32, 1536), BF16),...  74.2 us
    unnamed x4, local copies, waits for them, and re-layouts  1.89 us

profile of v4, /device:TPU:2, one launch (start us, length us, event | category | flops | bytes accessed | tf_op | source)
XLA Modules:
  0.0 77.4 jit_solution(10437802273171121421)
XLA Ops:
  1.3 0.0 copy-start
  1.3 0.6 copy-done
  1.9 74.2 %shard_map.122 = (bf16[32,1536]{1,0:T(8,128)(2,1)S(1)}, bf16[4,1536]{1,0:T(4,128)(2,1)S(1)}) custom-call(s32[1]{0:T(128)S(6)} %copy.15.timestep, s32[4]{0:T(128)S(1)} %copy-done, bf16[32,1536]{1,0:T(8,128)(2,1)} %latent.1, bf16[4,1536]{1,0:T(4,128)(2,1)} %text.1, bf16[32,1536]{1,0:T(8,128)(2,1)} %bitcast.24, bf16[4,1536]{1,0:T(4,128)(2,1)} %bitcast.25, ...), custom_call_target="tpu_custom_call" | custom-call | tf_op jit(solution)/shard_map/pallas_call | solution.py:584
  76.2 0.6 copy.16
  76.8 0.6 copy.17
Async XLA Ops:
  1.3 0.7 copy-start

commit v5 on v4

--- a/solution.py
+++ b/solution.py
@@ -132,7 +132,7 @@
         arrived(zv.at[zz], r_z.at[d, 0])
         slot = zz * 4 + y
         tokv[slot] = normed(zv[zz].astype(F32), 0)
-        for e in (1, 3, 2):
+        for e in (2, 1, 3):
             copy_to(tokv.at[slot], tokv.at[slot], r_y.at[e - 1, d], ypeer(e))
 
     norm_piece(0)
@@ -140,7 +140,7 @@
         arrived(zt.at[(z + 4 - d) % 4], r_z.at[d, 1])
     rows = jnp.concatenate([unpack(zt[j].astype(F32)) for j in range(4)], axis=0)
     tokt[y] = normed(rows, 1)
-    for e in (1, 3, 2):
+    for e in (2, 1, 3):
         copy_to(tokt.at[y], tokt.at[y], r_y.at[e - 1, 4], ypeer(e))
     norm_piece(1)
     norm_piece(3)
@@ -181,7 +181,7 @@
         ).astype(BF16)
 
     def set_keys(ch):
-        for e in (1, 3, 2):
+        for e in (2, 1, 3):
             arrived(kv.at[ch, 0], r_kv.at[e - 1, ch])
         keys = by_rows([kv[ch, yy, 0:96] for yy in range(4)])
         values = by_rows([kv[ch, yy, 96:192] for yy in range(4)])
@@ -204,7 +204,7 @@
     def video_chunk(k):
         d = order[k]
         zz = (z + 4 - d) % 4
-        for e in (1, 3, 2):
+        for e in (2, 1, 3):
             arrived(tokv.at[zz * 4 + (y + 4 - e) % 4], r_y.at[e - 1, d])
         b[k] = project(tokv[pl.ds(zz * 4, 4)].reshape(128, 1536), 0)
 
@@ -216,7 +216,7 @@
         def _():
             query_send(k, zz).start()
 
-        for e in (1, 3, 2):
+        for e in (2, 1, 3):
             copy_to(b.at[k, 96:288], kv.at[k, y], r_kv.at[e - 1, k], ypeer(e))
         kv[k, y] = b[k, 96:288]
 
@@ -255,7 +255,7 @@
     for d in (1, 3, 2):
         arrived(wq.at[(x + 4 - d) % 4, pl.ds(80, 64)], r_w.at[d - 1, 1])
     regroup(1)
-    for e in (1, 3, 2):
+    for e in (2, 1, 3):
         arrived(tokt.at[(y + 4 - e) % 4], r_y.at[e - 1, 4])
     b[4] = project(tokt[...].reshape(128, 1536), 1)
     to_diag = (y + 4 - x) % 4
@@ -276,7 +276,7 @@
     def _():
         text_query().start()
 
-    for e in (1, 3, 2):
+    for e in (2, 1, 3):
         copy_to(b.at[4, 96:288], kv.at[4, y], r_kv.at[e - 1, 4], ypeer(e))
     kv[4, y] = b[4, 96:288]
 

time: 77.5 us -> 77.2 us (level)
  no operation moved by 1% of the time
where the time goes in v5:
time: 77.2 us; the launch traced here: 77 us
  Pallas kernels  73.8 us (96%)
  local copies, waits for them, and re-layouts  1.89 us (2%)
  between operations  1.3 us (2%)
    pallas_call x1, Pallas kernels, body(): pl.pallas_call(kernel, out_shape=(jax.ShapeDtypeStruct((32, 1536), BF16),...  73.8 us
    unnamed x4, local copies, waits for them, and re-layouts  1.89 us

profile of v5, /device:TPU:2, one launch (start us, length us, event | category | flops | bytes accessed | tf_op | source)
XLA Modules:
  0.0 77.0 jit_solution(6696003078884290241)
XLA Ops:
  1.3 0.0 copy-start
  1.3 0.6 copy-done
  1.9 73.8 %shard_map.122 = (bf16[32,1536]{1,0:T(8,128)(2,1)S(1)}, bf16[4,1536]{1,0:T(4,128)(2,1)S(1)}) custom-call(s32[1]{0:T(128)S(6)} %copy.15.timestep, s32[4]{0:T(128)S(1)} %copy-done, bf16[32,1536]{1,0:T(8,128)(2,1)} %latent.1, bf16[4,1536]{1,0:T(4,128)(2,1)} %text.1, bf16[32,1536]{1,0:T(8,128)(2,1)} %bitcast.24, bf16[4,1536]{1,0:T(4,128)(2,1)} %bitcast.25, ...), custom_call_target="tpu_custom_call" | custom-call | tf_op jit(solution)/shard_map/pallas_call | solution.py:584
  75.7 0.6 copy.16
  76.4 0.6 copy.17
Async XLA Ops:
  1.3 0.7 copy-start
